TPU v7x, 256 devices: a whole 4x4x8 slice. The times are simulated.
256 devices in a mesh: order: 32 (over y_hi, z, core), member: 8 (over y_lo, x).
Axes of the slice: x: 4, y: 4 (y_hi: 2, y_lo: 2; y = y_hi * 2 + y_lo), z: 8, core: 2. Of those that a mesh axis runs over, the one named last changes fastest.
Arguments:
- members: bfloat16 [32, 384, 8, 2, 768], P('member', 'order'), may hold values from -5000 to 5000
- observed: bfloat16 [384, 8, 2, 768], P('order'), may hold values from -2000 to 2000
- pair_order: int32 [384], P('order'), may hold values from -1 to 360, as said below
- degree_weight: float32 [721], replicated, may hold values from 0.25 to 4
- cotangent: float32 [8], replicated, may hold values from 0.5 to 2
Outputs:
- member_grad: float32 [32, 384, 8, 2, 768], P('member', 'order')
Inputs may be any that keep to these rules, and one draw needn't show every extreme that they name: `pair_order`: every shorter order 0 to 360 stands in exactly one row; the other 23 rows hold -1.
All inputs are finite; a program needn't handle non-finite values.
Results may differ from a plain program's by a relative error of at most 0.0012.
Values may be sent and summed in bfloat16 or wider, within the bound.
No kernel may reach another device: no remote copies, remote signals or barrier semaphores. Data moves between devices by JAX's collectives and lax.ppermute only.
A program may use at most 64 MiB of HBM per device.

v0:
```python
import jax
import jax.numpy as jnp
from jax import lax
from jax.sharding import PartitionSpec as P

epsilon = 1e-06


def from_behind(shard, axis, by):
    length = lax.axis_size(axis)
    return lax.ppermute(shard, axis, [(i, (i + by) % length) for i in range(length)])


def slot_weights(pair_order, degree_weight, slot_count):
    degrees = degree_weight.shape[0]
    slot_index = lax.broadcasted_iota(jnp.int32, (pair_order.shape[0], slot_count), 1)
    shorter = pair_order[:, None]
    leading = slot_index < degrees - shorter
    padded = jnp.concatenate([degree_weight, jnp.zeros((slot_count,), jnp.float32)])
    starts = jnp.maximum(pair_order, 0)
    head_part = jax.vmap(lambda start: lax.dynamic_slice_in_dim(padded, start, slot_count))(starts)
    tail_part = jnp.concatenate(
        [
            jnp.zeros((1,), jnp.float32),
            degree_weight,
            jnp.zeros((slot_count - degrees - 1,), jnp.float32),
        ]
    )[None, :]
    usable = (shorter >= 0) & (leading | (slot_index <= degrees) & (2 * shorter < degrees - 1))
    multiplicity = jnp.where(leading & (shorter == 0), 1.0, 2.0)
    return jnp.where(usable, jnp.where(leading, head_part, tail_part) * multiplicity, 0.0)


def blocks_behind(block, steps_count):
    received = []
    for step_index in range(steps_count):
        block = from_behind(block, "member", 1)
        received.append(block)
    return received


def block_partial(own_block, other_block, weights):
    leading = own_block.astype(jnp.float32)
    partner = other_block.astype(jnp.float32)
    results = []
    for row_index in range(leading.shape[0]):
        difference = leading[row_index][None] - partner
        results.append(jnp.sum(weights * difference * difference, axis=(1, 3, 4)))
    return jnp.stack(results)


def block_pull(own_block, other_block, factor):
    leading = own_block.astype(jnp.float32)
    partner = other_block.astype(jnp.float32)
    results = []
    for row_index in range(leading.shape[0]):
        difference = leading[row_index][None] - partner
        results.append(jnp.sum(factor[row_index][:, None, :, None, None] * difference, axis=0))
    return jnp.stack(results)


def cycle_gradient(members, observed, weights, degree_weight, cotangent, blocks, total_members):
    local_count = members.shape[0]
    target = observed.astype(jnp.float32)
    own_block = members.astype(jnp.float32)
    target_diff = own_block - target[None]
    target_part = jnp.sum(weights[None] * target_diff * target_diff, axis=(1, 3, 4))
    partials = [block_partial(members, other_block, weights) for other_block, is_self in blocks]
    first_sq, target_sq = lax.psum((partials[0], target_part), "order")
    pair_sq = [first_sq] + [lax.psum(partial_term, "order") for partial_term in partials[1:]]
    diagonal = jnp.eye(local_count, dtype=jnp.float32)[:, :, None]
    pulled = jnp.zeros_like(own_block)
    for (other_block, is_self), squared in zip(blocks, pair_sq):
        keep_mask = 1.0 - diagonal * jnp.asarray(is_self).astype(jnp.float32)
        factor = keep_mask / jnp.sqrt(squared + epsilon) / (total_members - 1)
        pulled = pulled + block_pull(members, other_block, factor)
    target_dist = jnp.sqrt(target_sq + epsilon)
    toward = target_diff / target_dist[:, None, :, None, None]
    degrees = degree_weight.shape[0]
    return degrees * cotangent[None, None, :, None, None] * weights[None] * (toward - pulled)


def on_device(members, observed, pair_order, degree_weight, cotangent):
    weights = slot_weights(pair_order, degree_weight, members.shape[-1])[:, None, None, :]
    groups = lax.axis_size("member")
    local_count = members.shape[0]
    total_members = local_count * groups
    blocks = [(members, True)] + [
        (received, False) for received in blocks_behind(members, groups - 1)
    ]
    gradient = cycle_gradient(
        members, observed, weights, degree_weight, cotangent, blocks, total_members
    )
    return gradient


def solution(mesh):
    placed = (
        P("member", "order", None, None, None),
        P("order", None, None, None),
        P("order"),
        P(),
        P(),
    )
    return jax.shard_map(
        on_device,
        mesh=mesh,
        in_specs=placed,
        out_specs=P("member", "order", None, None, None),
        check_vma=False,
    )
```

profile of v0, /device:TPU:8, one launch (start us, length us, event | category | flops | bytes accessed | tf_op | source)
XLA Modules:
  0.0 516.9 jit_solution(2229843598273610351)
XLA Ops:
  0.0 1.6 collective-permute-start
  1.6 28.5 %collective-permute-done = bf16[4,12,8,2,768]{4,3,2,1,0:T(2,128)(2,1)S(1)} collective-permute-done((bf16[4,12,8,2,768]{4,3,2,1,0:T(2,128)(2,1)}, bf16[4,12,8,2,768]{4,3,2,1,0:T(2,128)(2,1)S(1)}, u32[]{:S(2)}, u32[]{:S(2)}) %collective-permute-start) | collective-permute-done | bytes 1179680 | tf_op jit(solution)/shard_map/ppermute | solution.py:11
  30.1 1.0 copy-done.12
  31.2 27.9 %collective-permute-done.1 = bf16[4,12,8,2,768]{4,3,2,1,0:T(2,128)(2,1)S(1)} collective-permute-done((bf16[4,12,8,2,768]{4,3,2,1,0:T(2,128)(2,1)S(1)}, bf16[4,12,8,2,768]{4,3,2,1,0:T(2,128)(2,1)S(1)}, u32[]{:S(2)}, u32[]{:S(2)}) %collective-permute-start.1) | collective-permute-done | bytes 1179680 | tf_op jit(solution)/shard_map/ppermute | solution.py:11
  59.1 1.0 copy-done.14
  60.1 27.0 %collective-permute-done.2 = bf16[4,12,8,2,768]{4,3,2,1,0:T(2,128)(2,1)S(1)} collective-permute-done((bf16[4,12,8,2,768]{4,3,2,1,0:T(2,128)(2,1)S(1)}, bf16[4,12,8,2,768]{4,3,2,1,0:T(2,128)(2,1)S(1)}, u32[]{:S(2)}, u32[]{:S(2)}) %collective-permute-start.2) | collective-permute-done | bytes 1179680 | tf_op jit(solution)/shard_map/ppermute | solution.py:11
  87.1 1.0 copy-done.4
  88.1 27.1 %collective-permute-done.3 = bf16[4,12,8,2,768]{4,3,2,1,0:T(2,128)(2,1)S(1)} collective-permute-done((bf16[4,12,8,2,768]{4,3,2,1,0:T(2,128)(2,1)S(1)}, bf16[4,12,8,2,768]{4,3,2,1,0:T(2,128)(2,1)S(1)}, u32[]{:S(2)}, u32[]{:S(2)}) %collective-permute-start.3) | collective-permute-done | bytes 1179680 | tf_op jit(solution)/shard_map/ppermute | solution.py:11
  115.2 1.0 copy-done.7
  116.3 26.2 %collective-permute-done.4 = bf16[4,12,8,2,768]{4,3,2,1,0:T(2,128)(2,1)S(1)} collective-permute-done((bf16[4,12,8,2,768]{4,3,2,1,0:T(2,128)(2,1)S(1)}, bf16[4,12,8,2,768]{4,3,2,1,0:T(2,128)(2,1)S(1)}, u32[]{:S(2)}, u32[]{:S(2)}) %collective-permute-start.4) | collective-permute-done | bytes 1179680 | tf_op jit(solution)/shard_map/ppermute | solution.py:11
  142.5 4.4 convert_element_type.25
  146.9 1.1 convert_element_type.26
  148.0 17.0 %while.2 = (s32[]{:T(128)}, f32[1489]{0:T(1024)S(1)}, s32[12,1]{0,1:T(1,128)S(1)}, f32[12,768]{1,0:T(8,128)S(1)}) while((s32[]{:T(128)}, f32[1489]{0:T(1024)S(1)}, s32[12,1]{0,1:T(1,128)S(1)}, f32[12,768]{1,0:T(8,128)S(1)}) %tuple.249), condition=%wide.while_cond.clone, body=%wide.while_body.sunk.clone | while | flops 2 | bytes 18505 | solution.py:21
  148.0 0.6 constant_dynamic-slice_fusion.3
  148.6 0.7 dynamic-slice.9
  149.4 0.6 constant_dynamic-slice_fusion.3
  150.1 0.7 dynamic-slice.9
  150.8 0.6 constant_dynamic-slice_fusion.3
  151.5 0.7 dynamic-slice.9
  152.3 0.6 constant_dynamic-slice_fusion.3
  152.9 0.7 dynamic-slice.9
  153.7 0.6 constant_dynamic-slice_fusion.3
  154.3 0.7 dynamic-slice.9
  155.1 0.6 constant_dynamic-slice_fusion.3
  155.7 0.7 dynamic-slice.9
  157.1 0.7 dynamic-slice.9
  158.6 0.7 dynamic-slice.9
  159.3 0.6 constant_dynamic-slice_fusion.3
  160.0 0.7 dynamic-slice.9
  160.8 0.6 constant_dynamic-slice_fusion.3
  161.4 0.7 dynamic-slice.9
  162.8 0.7 dynamic-slice.9
  164.2 0.7 dynamic-slice.9
  165.7 2.7 collective-permute-done.5
  168.5 0.8 broadcast_multiply_fusion
  169.3 2.6 slice_bitcast_fusion.1
  172.0 21.0 %collective-permute-done.6 = bf16[4,12,8,2,768]{4,3,2,1,0:T(2,128)(2,1)S(1)} collective-permute-done((bf16[4,12,8,2,768]{4,3,2,1,0:T(2,128)(2,1)}, bf16[4,12,8,2,768]{4,3,2,1,0:T(2,128)(2,1)S(1)}, u32[]{:S(2)}, u32[]{:S(2)}) %collective-permute-start.6) | collective-permute-done | bytes 1179680 | tf_op jit(solution)/shard_map/ppermute | solution.py:11
  193.0 104.5 %fusion.100 = (f32[4,8]{1,0:T(4,128)S(1)}, f32[4,8]{1,0:T(4,128)S(1)}, f32[4,8]{1,0:T(4,128)S(1)}, f32[4,8]{1,0:T(4,128)S(1)}, f32[4,8]{1,0:T(4,128)S(1)}, /*ind...) fusion(bf16[4,12,8,2,768]{4,3,2,1,0:T(2,128)(2,1)S(1)} %collect, ...), kind=kLoop, calls=%fused_computation.169 | loop fusion | flops 82574304 | bytes 12427392 | tf_op jit(solution)/shard_map/reduce_sum | solution.py:48
  301.1 132.2 %all-reduce.1 = (f32[4,4,8]{2,1,0:T(4,128)}, f32[4,4,8]{2,1,0:T(4,128)}, f32[4,4,8]{2,1,0:T(4,128)}, f32[4,4,8]{2,1,0:T(4,128)}, f32[4,4,8]{2,1,0:T(4,128)}, /*i...) all-reduce(f32[4,4,8]{2,1,0:T(4,128)} %pad_maximum_fusion.7, ...), channel_id=1, replica_groups=mesh['order'=32,'member'=8] {'order'}, use_global_device_ids=true, to_apply=%region_69.70 | all-reduce | flops 1056 | bytes 8448 | tf_op jit(solution)/shard_map/psum | solution.py:70
  433.3 0.8 rsqrt_multiply_fusion.6
  434.1 0.7 rsqrt_multiply_fusion.4
  434.9 0.7 rsqrt_multiply_fusion.2
  436.3 0.7 rsqrt_multiply_fusion
  437.0 0.7 add_sqrt_fusion
  437.7 17.2 %fusion.37 = (f32[12,8,2,768]{3,2,1,0:T(2,128)}, f32[12,8,2,768]{3,2,1,0:T(2,128)}, f32[12,8,2,768]{3,2,1,0:T(2,128)}, f32[12,8,2,768]{3,2,1,0:T(2,128)}, f32[12...) fusion(bf16[4,12,8,2,768]{4,3,2,1,0:T(2,128)(2,1)} %copy-done.3, ...), kind=kLoop, calls=%fused_computation.104 | loop fusion | flops 14155776 | bytes 9438208 | tf_op jit(solution)/shard_map/reduce_sum | solution.py:58
  454.9 25.7 %fusion.57 = (f32[12,8,2,768]{3,2,1,0:T(2,128)S(1)}, f32[12,8,2,768]{3,2,1,0:T(2,128)S(1)}, f32[12,8,2,768]{3,2,1,0:T(2,128)S(1)}, f32[12,8,2,768]{3,2,1,0:T(2,1...) fusion(bf16[4,12,8,2,768]{4,3,2,1,0:T(2,128)(2,1)} %copy-done.1, ...), kind=kLoop, calls=%fused_computation.124 | loop fusion | flops 21233664 | bytes 12977664 | tf_op jit(solution)/shard_map/reduce_sum | solution.py:58
  480.8 24.5 %fusion.45 = (f32[12,8,2,768]{3,2,1,0:T(2,128)S(1)}, f32[12,8,2,768]{3,2,1,0:T(2,128)S(1)}, f32[12,8,2,768]{3,2,1,0:T(2,128)}, f32[12,8,2,768]{3,2,1,0:T(2,128)}...) fusion(bf16[4,12,8,2,768]{4,3,2,1,0:T(2,128)(2,1)S(1)} %copy-do, ...), kind=kLoop, calls=%fused_computation.112 | loop fusion | flops 21233664 | bytes 12977664 | tf_op jit(solution)/shard_map/reduce_sum | solution.py:58
  505.4 11.3 %fusion.104 = f32[4,12,8,2,768]{4,3,2,1,0:T(2,128)} fusion(f32[1,12,8,2,768]{4,3,2,1,0:T(2,128)S(1)} %bitcast.149, f32[1,12,8,2,768]{4,3,2,1,0:T(2,128)S(1)} %bitcast.148, f32[1,12,8,2,768]{4,3,2,1,0:T(2,128)S(1)} %bitcast.143, f32[1,12,8,2,768]{4,3,2,1,0:T(2,128)S(1)} %bitcast.142, bf16[4,12,8,2,768]{4,3,2,1,0:T(2,128)(2,1)S(1)} %copy-done, ...), kind=kLoop, calls=%fused_computation.173 | loop fusion | flops 21233664 | bytes 23298176 | tf_op jit(solution)/shard_map/mul | solution.py:80
  (120 shorter events, 8.4 us)
Async XLA Ops:
  0.0 146.9 %copy-start.25 = (bf16[12,8,2,768]{3,2,1,0:T(2,128)(2,1)S(1)}, bf16[12,8,2,768]{3,2,1,0:T(2,128)(2,1)}, u32[]{:S(2)}) copy-start(bf16[12,8,2,768]{3,2,1,0:T(2,128)(2,1)} %param.6) | copy-start | bytes 884740
  0.0 148.0 %copy-start.26 = (f32[721]{0:T(1024)S(1)}, f32[721]{0:T(1024)}, u32[]{:S(2)}) copy-start(f32[721]{0:T(1024)} %param.8) | copy-start | bytes 8656
  0.0 148.0 %copy-start.30 = (s32[12]{0:T(128)S(1)}, s32[12]{0:T(128)}, u32[]{:S(2)}) copy-start(s32[12]{0:T(128)} %param.7) | copy-start | bytes 148
  0.0 168.4 %copy-start.31 = (f32[8]{0:T(128)S(1)}, f32[8]{0:T(128)}, u32[]{:S(2)}) copy-start(f32[8]{0:T(128)} %param.9) | copy-start | bytes 100
  0.0 30.1 %collective-permute-start = (bf16[4,12,8,2,768]{4,3,2,1,0:T(2,128)(2,1)}, bf16[4,12,8,2,768]{4,3,2,1,0:T(2,128)(2,1)S(1)}, u32[]{:S(2)}, u32[]{:S(2)}) collective-permute-start(bf16[4,12,8,2,768]{4,3,2,1,0:T(2,128)(2,1)} %param.5), channel_id=1, source_target_pairs={{0,1},{1,2},{2,3},{3,4},{4,5},{5,6},{6,7},{7,0},{8,9},{9,10},{10,1... | collective-permute-start | bytes 3538952 | tf_op jit(solution)/shard_map/ppermute | solution.py:11
  30.1 1.1 copy-start.12
  30.1 28.9 %collective-permute-start.1 = (bf16[4,12,8,2,768]{4,3,2,1,0:T(2,128)(2,1)S(1)}, bf16[4,12,8,2,768]{4,3,2,1,0:T(2,128)(2,1)S(1)}, u32[]{:S(2)}, u32[]{:S(2)}) collective-permute-start(bf16[4,12,8,2,768]{4,3,2,1,0:T(2,128)(2,1)S(1)} %collective-permute-done), channel_id=1, source_target_pairs={{0,1},{1,2},{2,3},{3,4},{4,5},{5,6},{6,7},{7,0},{8,9},{9,10},{10,1... | collective-permute-start | bytes 3538952 | tf_op jit(solution)/shard_map/ppermute | solution.py:11
  59.1 1.0 copy-start.14
  59.1 28.0 %collective-permute-start.2 = (bf16[4,12,8,2,768]{4,3,2,1,0:T(2,128)(2,1)S(1)}, bf16[4,12,8,2,768]{4,3,2,1,0:T(2,128)(2,1)S(1)}, u32[]{:S(2)}, u32[]{:S(2)}) collective-permute-start(bf16[4,12,8,2,768]{4,3,2,1,0:T(2,128)(2,1)S(1)} %collective-permute-done.1), channel_id=1, source_target_pairs={{0,1},{1,2},{2,3},{3,4},{4,5},{5,6},{6,7},{7,0},{8,9},{9,10},{10,1... | collective-permute-start | bytes 3538952 | tf_op jit(solution)/shard_map/ppermute | solution.py:11
  87.1 1.0 copy-start.4
  88.1 27.1 %collective-permute-start.3 = (bf16[4,12,8,2,768]{4,3,2,1,0:T(2,128)(2,1)S(1)}, bf16[4,12,8,2,768]{4,3,2,1,0:T(2,128)(2,1)S(1)}, u32[]{:S(2)}, u32[]{:S(2)}) collective-permute-start(bf16[4,12,8,2,768]{4,3,2,1,0:T(2,128)(2,1)S(1)} %collective-permute-done.2), channel_id=1, source_target_pairs={{0,1},{1,2},{2,3},{3,4},{4,5},{5,6},{6,7},{7,0},{8,9},{9,10},{10,1... | collective-permute-start | bytes 3538952 | tf_op jit(solution)/shard_map/ppermute | solution.py:11
  115.2 1.1 copy-start.7
  116.3 26.2 %collective-permute-start.4 = (bf16[4,12,8,2,768]{4,3,2,1,0:T(2,128)(2,1)S(1)}, bf16[4,12,8,2,768]{4,3,2,1,0:T(2,128)(2,1)S(1)}, u32[]{:S(2)}, u32[]{:S(2)}) collective-permute-start(bf16[4,12,8,2,768]{4,3,2,1,0:T(2,128)(2,1)S(1)} %collective-permute-done.3), channel_id=1, source_target_pairs={{0,1},{1,2},{2,3},{3,4},{4,5},{5,6},{6,7},{7,0},{8,9},{9,10},{10,1... | collective-permute-start | bytes 3538952 | tf_op jit(solution)/shard_map/ppermute | solution.py:11
  142.5 26.1 %copy-start.10 = (bf16[4,12,8,2,768]{4,3,2,1,0:T(2,128)(2,1)}, bf16[4,12,8,2,768]{4,3,2,1,0:T(2,128)(2,1)S(1)}, u32[]{:S(2)}) copy-start(bf16[4,12,8,2,768]{4,3,2,1,0:T(2,128)(2,1)S(1)} %collective-permute-done.4) | copy-start | bytes 3538948
  142.5 25.9 %collective-permute-start.5 = (bf16[4,12,8,2,768]{4,3,2,1,0:T(2,128)(2,1)S(1)}, bf16[4,12,8,2,768]{4,3,2,1,0:T(2,128)(2,1)}, u32[]{:S(2)}, u32[]{:S(2)}) collective-permute-start(bf16[4,12,8,2,768]{4,3,2,1,0:T(2,128)(2,1)S(1)} %collective-permute-done.4), channel_id=1, source_target_pairs={{0,1},{1,2},{2,3},{3,4},{4,5},{5,6},{6,7},{7,0},{8,9},{9,10},{10,1... | collective-permute-start | bytes 3538952 | tf_op jit(solution)/shard_map/ppermute | solution.py:11
  168.4 24.6 %collective-permute-start.6 = (bf16[4,12,8,2,768]{4,3,2,1,0:T(2,128)(2,1)}, bf16[4,12,8,2,768]{4,3,2,1,0:T(2,128)(2,1)S(1)}, u32[]{:S(2)}, u32[]{:S(2)}) collective-permute-start(bf16[4,12,8,2,768]{4,3,2,1,0:T(2,128)(2,1)} %collective-permute-done.5), channel_id=1, source_target_pairs={{0,1},{1,2},{2,3},{3,4},{4,5},{5,6},{6,7},{7,0},{8,9},{9,10},{10,1... | collective-permute-start | bytes 3538952 | tf_op jit(solution)/shard_map/ppermute | solution.py:11
  169.3 23.7 %copy-start = (bf16[4,12,8,2,768]{4,3,2,1,0:T(2,128)(2,1)S(1)}, bf16[4,12,8,2,768]{4,3,2,1,0:T(2,128)(2,1)}, u32[]{:S(2)}) copy-start(bf16[4,12,8,2,768]{4,3,2,1,0:T(2,128)(2,1)} %param.5) | copy-start | bytes 3538948
  169.3 23.7 %copy-start.1 = (f32[12,8,2,768]{3,2,1,0:T(2,128)S(1)}, f32[12,8,2,768]{3,2,1,0:T(2,128)}, u32[]{:S(2)}) copy-start(f32[12,8,2,768]{3,2,1,0:T(2,128)} %convert_element_type.26) | copy-start | bytes 1769476
  169.3 23.7 %copy-start.5 = (bf16[4,12,8,2,768]{4,3,2,1,0:T(2,128)(2,1)S(1)}, bf16[4,12,8,2,768]{4,3,2,1,0:T(2,128)(2,1)}, u32[]{:S(2)}) copy-start(bf16[4,12,8,2,768]{4,3,2,1,0:T(2,128)(2,1)} %copy-done.4) | copy-start | bytes 3538948
  169.3 23.7 %copy-start.8 = (bf16[4,12,8,2,768]{4,3,2,1,0:T(2,128)(2,1)S(1)}, bf16[4,12,8,2,768]{4,3,2,1,0:T(2,128)(2,1)}, u32[]{:S(2)}) copy-start(bf16[4,12,8,2,768]{4,3,2,1,0:T(2,128)(2,1)} %copy-done.7) | copy-start | bytes 3538948
  193.0 104.5 %copy-start.3 = (bf16[4,12,8,2,768]{4,3,2,1,0:T(2,128)(2,1)}, bf16[4,12,8,2,768]{4,3,2,1,0:T(2,128)(2,1)S(1)}, u32[]{:S(2)}) copy-start(bf16[4,12,8,2,768]{4,3,2,1,0:T(2,128)(2,1)S(1)} %collective-permute-done.6) | copy-start | bytes 3538948
  437.7 17.2 %copy-start.13 = (bf16[4,12,8,2,768]{4,3,2,1,0:T(2,128)(2,1)S(1)}, bf16[4,12,8,2,768]{4,3,2,1,0:T(2,128)(2,1)}, u32[]{:S(2)}) copy-start(bf16[4,12,8,2,768]{4,3,2,1,0:T(2,128)(2,1)} %copy-done.12) | copy-start | bytes 3538948
  454.9 25.7 %copy-start.6 = (bf16[4,12,8,2,768]{4,3,2,1,0:T(2,128)(2,1)S(1)}, bf16[4,12,8,2,768]{4,3,2,1,0:T(2,128)(2,1)}, u32[]{:S(2)}) copy-start(bf16[4,12,8,2,768]{4,3,2,1,0:T(2,128)(2,1)} %copy-done.4) | copy-start | bytes 3538948
  454.9 25.7 %copy-start.9 = (bf16[4,12,8,2,768]{4,3,2,1,0:T(2,128)(2,1)S(1)}, bf16[4,12,8,2,768]{4,3,2,1,0:T(2,128)(2,1)}, u32[]{:S(2)}) copy-start(bf16[4,12,8,2,768]{4,3,2,1,0:T(2,128)(2,1)} %copy-done.7) | copy-start | bytes 3538948
  454.9 25.7 %copy-start.11 = (bf16[4,12,8,2,768]{4,3,2,1,0:T(2,128)(2,1)S(1)}, bf16[4,12,8,2,768]{4,3,2,1,0:T(2,128)(2,1)}, u32[]{:S(2)}) copy-start(bf16[4,12,8,2,768]{4,3,2,1,0:T(2,128)(2,1)} %copy-done.10) | copy-start | bytes 3538948
  454.9 25.7 %copy-start.27 = (f32[4,8]{1,0:T(4,128)S(1)}, f32[4,8]{1,0:T(4,128)}, u32[]{:S(2)}) copy-start(f32[4,8]{1,0:T(4,128)} %get-tuple-element.263) | copy-start | bytes 388
  454.9 25.7 %copy-start.28 = (f32[4,8]{1,0:T(4,128)S(1)}, f32[4,8]{1,0:T(4,128)}, u32[]{:S(2)}) copy-start(f32[4,8]{1,0:T(4,128)} %get-tuple-element.264) | copy-start | bytes 388
  454.9 25.7 %copy-start.29 = (f32[4,8]{1,0:T(4,128)S(1)}, f32[4,8]{1,0:T(4,128)}, u32[]{:S(2)}) copy-start(f32[4,8]{1,0:T(4,128)} %get-tuple-element.265) | copy-start | bytes 388
  480.7 24.7 %copy-start.2 = (f32[12,8,2,768]{3,2,1,0:T(2,128)S(1)}, f32[12,8,2,768]{3,2,1,0:T(2,128)}, u32[]{:S(2)}) copy-start(f32[12,8,2,768]{3,2,1,0:T(2,128)} %convert_element_type.26) | copy-start | bytes 1769476
  480.7 24.6 %copy-start.15 = (f32[12,8,2,768]{3,2,1,0:T(2,128)S(1)}, f32[12,8,2,768]{3,2,1,0:T(2,128)}, u32[]{:S(2)}) copy-start(f32[12,8,2,768]{3,2,1,0:T(2,128)} %get-tuple-element.217) | copy-start | bytes 1769476
  480.7 24.6 %copy-start.16 = (f32[12,8,2,768]{3,2,1,0:T(2,128)S(1)}, f32[12,8,2,768]{3,2,1,0:T(2,128)}, u32[]{:S(2)}) copy-start(f32[12,8,2,768]{3,2,1,0:T(2,128)} %get-tuple-element.218) | copy-start | bytes 1769476
  480.7 24.6 %copy-start.17 = (f32[12,8,2,768]{3,2,1,0:T(2,128)S(1)}, f32[12,8,2,768]{3,2,1,0:T(2,128)}, u32[]{:S(2)}) copy-start(f32[12,8,2,768]{3,2,1,0:T(2,128)} %get-tuple-element.219) | copy-start | bytes 1769476
  480.7 24.6 %copy-start.18 = (f32[12,8,2,768]{3,2,1,0:T(2,128)S(1)}, f32[12,8,2,768]{3,2,1,0:T(2,128)}, u32[]{:S(2)}) copy-start(f32[12,8,2,768]{3,2,1,0:T(2,128)} %get-tuple-element.220) | copy-start | bytes 1769476
  480.7 24.6 %copy-start.19 = (f32[12,8,2,768]{3,2,1,0:T(2,128)S(1)}, f32[12,8,2,768]{3,2,1,0:T(2,128)}, u32[]{:S(2)}) copy-start(f32[12,8,2,768]{3,2,1,0:T(2,128)} %get-tuple-element.221) | copy-start | bytes 1769476
  480.7 24.6 %copy-start.20 = (f32[12,8,2,768]{3,2,1,0:T(2,128)S(1)}, f32[12,8,2,768]{3,2,1,0:T(2,128)}, u32[]{:S(2)}) copy-start(f32[12,8,2,768]{3,2,1,0:T(2,128)} %get-tuple-element.222) | copy-start | bytes 1769476
  480.7 24.6 %copy-start.21 = (f32[12,8,2,768]{3,2,1,0:T(2,128)S(1)}, f32[12,8,2,768]{3,2,1,0:T(2,128)}, u32[]{:S(2)}) copy-start(f32[12,8,2,768]{3,2,1,0:T(2,128)} %get-tuple-element.223) | copy-start | bytes 1769476
  480.8 24.6 %copy-start.22 = (f32[12,8,2,768]{3,2,1,0:T(2,128)S(1)}, f32[12,8,2,768]{3,2,1,0:T(2,128)}, u32[]{:S(2)}) copy-start(f32[12,8,2,768]{3,2,1,0:T(2,128)} %get-tuple-element.224) | copy-start | bytes 1769476
  480.8 24.6 %copy-start.23 = (f32[12,8,2,768]{3,2,1,0:T(2,128)S(1)}, f32[12,8,2,768]{3,2,1,0:T(2,128)}, u32[]{:S(2)}) copy-start(f32[12,8,2,768]{3,2,1,0:T(2,128)} %get-tuple-element.188) | copy-start | bytes 1769476
  480.8 24.6 %copy-start.24 = (f32[12,8,768]{2,1,0:T(8,128)S(1)}, f32[12,8,768]{2,1,0:T(8,128)}, u32[]{:S(2)}) copy-start(f32[12,8,768]{2,1,0:T(8,128)} %broadcast_multiply_fusion) | copy-start | bytes 884740
where the time goes:
time: 518 us; the launch traced here: 517 us
  other arithmetic  198 us (38%)
  waiting for transfers between devices  160 us (31%)
  blocking collectives  132 us (25%)
  local copies, waits for them, and re-layouts  24.2 us (5%)
    ppermute x7, waiting for transfers between devices, from_behind(): lax.ppermute(shard, axis, [(i, (i + by) % length) for i in range(length)])  160 us
    psum x1, blocking collectives, cycle_gradient(): lax.psum(partial_term, 'order')  132 us
    reduce_sum x1, other arithmetic, block_partial(): results.append(jnp.sum(weights * difference * difference, axis=(1, 3, 4)))  104 us
    reduce_sum x3, other arithmetic, block_pull(): jnp.sum(factor[row_index][:, None, :, None, None] * difference, axis=0)  67.5 us
    gather x48, local copies, waits for them, and re-layouts  16.7 us
    mul x3, other arithmetic, cycle_gradient(): degrees * cotangent[None, None, :, None, None] * weights[None]  12.1 us
  transfers between devices with their start and end apart: 7, of which 7 were waited for; matrix products, arithmetic and copies ran while one was open for 5% of the time, Pallas kernels for 0%

commit v1 on v0

v1 whole, which is shorter than its diff:
```python
import functools

import jax
import jax.numpy as jnp
from jax import lax
from jax.experimental import pallas as pl
from jax.experimental.pallas import tpu as pltpu
from jax.sharding import PartitionSpec as P

epsilon = 1e-06
LANES = 128
GROUP = 4
BATCH = 32


def pair_table(count):
    groups = [list(range(g, g + GROUP)) for g in range(0, count, GROUP)]
    cross = [(a, b) for a in range(len(groups)) for b in range(a + 1, len(groups))]
    batches = []
    for at in range(0, len(cross), 2):
        batches.append([(m, n) for a, b in cross[at : at + 2] for m in groups[a] for n in groups[b]])
    for at in range(0, len(groups), 2):
        inner = [(m, n) for g in groups[at : at + 2] for i, m in enumerate(g) for n in g[i + 1 :]]
        batches.append(inner + [(m, count) for g in groups[at : at + 2] for m in g])
    place, start, starts = {}, 0, []
    for batch in batches:
        starts.append(start)
        for index, pair in enumerate(batch):
            place[pair] = start + index
        start += -(-len(batch) // 8) * 8
    return batches, starts, place, -(-start // LANES) * LANES


def fold_rows(blocks):
    row = lax.broadcasted_iota(jnp.int32, (8, LANES), 0)
    for half in (4, 2, 1):
        low = (row & half) == 0
        count = len(blocks) // 2
        merged = []
        for i in range(count):
            a, b = blocks[i], blocks[i + count]
            kept = jnp.where(low, a, b)
            moved = jnp.where(low, b, a)
            merged.append(kept + (pltpu.roll(moved, half, 0) if half == 4 else swap(moved, half, low)))
        blocks = merged
    return blocks[0]


def swap(block, half, low):
    return jnp.where(low, pltpu.roll(block, 8 - half, 0), pltpu.roll(block, half, 0))


def weights_kernel(degrees, order_ref, table_ref, out_ref):
    slots = table_ref.shape[1]
    parts = slots // LANES
    table = table_ref[...]
    slot = lax.broadcasted_iota(jnp.int32, table.shape, 1)
    tail = pltpu.roll(table, 1, 1)
    for row in range(order_ref.shape[0]):
        order = order_ref[row]
        head = pltpu.roll(table, lax.rem(slots - jnp.maximum(order, 0), slots), 1)
        leading = slot < degrees - order
        second = (slot <= degrees) & (2 * order < degrees - 1)
        usable = (order >= 0) & (leading | second)
        times = jnp.where(leading & (order == 0), 1.0, 2.0)
        line = jnp.where(usable, jnp.where(leading, head, tail) * times, 0.0)
        for part in range(parts):
            at = (row * parts + part) * 2
            out_ref[at : at + 2, :] = line[0:2, part * LANES : (part + 1) * LANES]


def distance_kernel(batches, starts, count, x_ref, y_ref, w_ref, out_ref, scaled_ref, sums_ref):
    rows = w_ref.shape[0]

    def scale(i, carry):
        at = pl.ds(pl.multiple_of(i * 16, 16), 16)
        root = jnp.sqrt(w_ref[at, :])
        for m in range(count):
            scaled_ref[m, at, :] = x_ref[m, at, :].astype(jnp.float32) * root
        scaled_ref[count, at, :] = y_ref[at, :].astype(jnp.float32) * root
        return carry

    lax.fori_loop(0, rows // 16, scale, 0)
    sums_ref[...] = jnp.zeros_like(sums_ref)
    for batch, start in zip(batches, starts):
        used = sorted({m for pair in batch for m in pair})

        def add(i, sums, batch=batch, used=used):
            at = pl.ds(pl.multiple_of(i * 8, 8), 8)
            held = {m: scaled_ref[m, at, :] for m in used}
            out = []
            for (m, n), total in zip(batch, sums):
                difference = held[m] - held[n]
                out.append(total + difference * difference)
            return tuple(out)

        zero = jnp.zeros((8, LANES), jnp.float32)
        sums = list(lax.fori_loop(0, rows // 8, add, (zero,) * len(batch)))
        sums += [zero] * (-len(sums) % 8)
        for at in range(0, len(sums), 8):
            sums_ref[start + at : start + at + 8, :] = fold_rows(sums[at : at + 8])
    out_ref[...] = jnp.zeros_like(out_ref)
    for block in range(sums_ref.shape[0] // LANES):
        square = sums_ref[block * LANES : (block + 1) * LANES, :].T
        out_ref[block : block + 1, :] = jnp.sum(square, axis=0, keepdims=True)


def gradient_kernel(place, count, got_ref, x_ref, y_ref, w_ref, c_ref, out_ref, table_ref, wide_ref, pull_ref):
    rows = w_ref.shape[0]
    squares = jnp.sum(got_ref[...], axis=0)
    inverse = lax.rsqrt(squares + epsilon)
    columns = inverse.T
    for block in range(table_ref.shape[0] // LANES):
        column = jnp.broadcast_to(columns[:, block : block + 1], (LANES, LANES))
        table_ref[block * LANES : (block + 1) * LANES, :] = column

    def entry(m, n):
        at = place[(min(m, n), max(m, n))]
        return jnp.broadcast_to(table_ref[at : at + 1, :], (16, LANES))

    def slab(i, carry):
        at = pl.ds(pl.multiple_of(i * 16, 16), 16)
        for m in range(count):
            wide_ref[m] = x_ref[m, at, :].astype(jnp.float32)
        target = y_ref[at, :].astype(jnp.float32)
        weight = w_ref[at, :] * c_ref[0]
        share = 1.0 / (count - 1)
        for first in range(0, count, GROUP):
            own = list(range(first, first + GROUP))
            held = [wide_ref[m] for m in own]
            if first == 0:
                pulls = [jnp.zeros((16, LANES), jnp.float32) for _ in own]
            else:
                pulls = [pull_ref[m] for m in own]
            for i_m in range(GROUP):
                for i_n in range(i_m + 1, GROUP):
                    term = entry(own[i_m], own[i_n]) * (held[i_m] - held[i_n])
                    pulls[i_m] += term
                    pulls[i_n] -= term
            for second in range(first + GROUP, count, GROUP):
                for n in range(second, second + GROUP):
                    partner = wide_ref[n]
                    back = jnp.zeros((16, LANES), jnp.float32) if first == 0 else pull_ref[n]
                    for i_m in range(GROUP):
                        term = entry(own[i_m], n) * (held[i_m] - partner)
                        pulls[i_m] += term
                        back -= term
                    pull_ref[n] = back
            for i_m in range(GROUP):
                toward = (held[i_m] - target) * entry(own[i_m], count)
                out_ref[own[i_m], at, :] = (weight * (toward - pulls[i_m] * share)).astype(out_ref.dtype)
        return carry

    lax.fori_loop(0, rows // 16, slab, 0)


def on_device(members, observed, pair_order, degree_weight, cotangent):
    groups = lax.axis_size("member")
    spread = lax.axis_size("order")
    local, lines, channels, parts, slots = members.shape
    count = local * groups
    tiles = slots // LANES
    rows = lines * parts * tiles
    degrees = degree_weight.shape[0]
    batches, starts, place, entries = pair_table(count)
    vmem = pltpu.CompilerParams(vmem_limit_bytes=48 << 20)

    table = jnp.broadcast_to(jnp.pad(degree_weight, (0, slots - degrees))[None], (8, slots))
    weights = pl.pallas_call(
        functools.partial(weights_kernel, degrees),
        out_shape=jax.ShapeDtypeStruct((rows, LANES), jnp.float32),
        in_specs=[pl.BlockSpec(memory_space=pltpu.SMEM), pl.BlockSpec(memory_space=pltpu.VMEM)],
        compiler_params=vmem,
        name="slot_weights",
    )(pair_order, table)

    channel = lax.axis_index("member")
    held = lax.all_to_all(members.transpose(2, 0, 1, 3, 4), "member", 0, 0, tiled=True)
    held = held.reshape(count, lines, parts, tiles, LANES).transpose(0, 1, 3, 2, 4).reshape(count, rows, LANES)
    target = lax.dynamic_index_in_dim(observed, channel, 1, keepdims=False)
    target = target.reshape(lines, parts, tiles, LANES).transpose(0, 2, 1, 3).reshape(rows, LANES)

    blocks = entries // LANES
    sums = pl.pallas_call(
        functools.partial(distance_kernel, batches, starts, count),
        out_shape=jax.ShapeDtypeStruct((8, LANES), jnp.float32),
        scratch_shapes=[
            pltpu.VMEM((count + 1, rows, LANES), jnp.float32),
            pltpu.VMEM((entries, LANES), jnp.float32),
        ],
        compiler_params=vmem,
        name="distances",
    )(held, target, weights)
    got = lax.all_to_all(jnp.broadcast_to(sums[None], (spread, 8, LANES)), "order", 0, 0, tiled=True)

    factor = lax.dynamic_slice_in_dim(cotangent, channel, 1) * degrees
    whole = pl.BlockSpec(memory_space=pltpu.VMEM)
    gradient = pl.pallas_call(
        functools.partial(gradient_kernel, place, count),
        out_shape=jax.ShapeDtypeStruct((count, rows, LANES), jnp.float32),
        in_specs=[whole, whole, whole, whole, pl.BlockSpec(memory_space=pltpu.SMEM)],
        scratch_shapes=[
            pltpu.VMEM((blocks * LANES, LANES), jnp.float32),
            pltpu.VMEM((count, 16, LANES), jnp.float32),
            pltpu.VMEM((count, 16, LANES), jnp.float32),
        ],
        compiler_params=vmem,
        name="gradients",
    )(got, held, target, weights, factor)

    back = gradient.reshape(groups, local, lines, tiles, parts, LANES).transpose(0, 1, 2, 4, 3, 5)
    back = lax.all_to_all(back.reshape(groups, local, lines, parts, slots), "member", 0, 0, tiled=True)
    return back.transpose(1, 2, 0, 3, 4)


def solution(mesh):
    placed = (
        P("member", "order", None, None, None),
        P("order", None, None, None),
        P("order"),
        P(),
        P(),
    )
    return jax.shard_map(
        on_device,
        mesh=mesh,
        in_specs=placed,
        out_specs=P("member", "order", None, None, None),
        check_vma=False,
    )
```

time: 518 us -> 105 us (0.20)
  other arithmetic: 198 us -> 0 us
  waiting for transfers between devices: 160 us -> 25.6 us
  blocking collectives: 132 us -> 32.1 us
  Pallas kernels: 0 us -> 15.1 us
  starting transfers between devices: 1.58 us -> 16.3 us
  local copies, waits for them, and re-layouts: 24.2 us -> 14.2 us
    reduce_sum x4 -> x0, other arithmetic: 172 us -> none  [the longest x1 104 us: block_partial(): results.append(jnp.sum(weights * difference * difference, axis=(1, 3, 4)))]
    ppermute x7 -> x0, waiting for transfers between devices: 160 us -> none  [from_behind(): lax.ppermute(shard, axis, [(i, (i + by) % length) for i in range(length)])]
    psum x1 -> x0, blocking collectives: 132 us -> none  [cycle_gradient(): lax.psum(partial_term, 'order')]
    all_to_all x0 -> x1, blocking collectives: none -> 32.1 us  [on_device(): lax.all_to_all(back.reshape(groups, local, lines, parts, slots), 'member'...]
    all_to_all x0 -> x2, waiting for transfers between devices: none -> 25.6 us  [the longest x1 14.8 us: on_device(): lax.all_to_all(members.transpose(2, 0, 1, 3, 4), 'member', 0, 0, tiled=True)]
    gather x48 -> x0, local copies, waits for them, and re-layouts: 16.7 us -> none
    all_to_all x0 -> x2, starting transfers between devices: none -> 16.3 us  [the longest x1 10.6 us: on_device(): lax.all_to_all(jnp.broadcast_to(sums[None], (spread, 8, LANES)), 'order',...]
    pallas_call x0 -> x3, Pallas kernels: none -> 15.1 us  [the longest x1 7.93 us: on_device(): pl.pallas_call(functools.partial(distance_kernel, batches, starts, count)...]
  transfers between devices with their start and end apart: 7 -> 2, of which waited for: 7 -> 2; matrix products, arithmetic and copies ran while one was open for 5% -> 1% of each run, Pallas kernels for 0% -> 1%
where the time goes in v1:
time: 105 us; the launch traced here: 104 us
  blocking collectives  32.1 us (31%)
  waiting for transfers between devices  25.6 us (24%)
  starting transfers between devices  16.3 us (16%)
  Pallas kernels  15.1 us (14%)
  local copies, waits for them, and re-layouts  14.2 us (14%)
    all_to_all x1, blocking collectives, on_device(): lax.all_to_all(back.reshape(groups, local, lines, parts, slots), 'member'...  32.1 us
    all_to_all x1, waiting for transfers between devices, on_device(): lax.all_to_all(members.transpose(2, 0, 1, 3, 4), 'member', 0, 0, tiled=True)  14.8 us
    all_to_all x1, waiting for transfers between devices, on_device(): lax.all_to_all(jnp.broadcast_to(sums[None], (spread, 8, LANES)), 'order',...  10.8 us
    all_to_all x1, starting transfers between devices, on_device(): lax.all_to_all(jnp.broadcast_to(sums[None], (spread, 8, LANES)), 'order',...  10.6 us
    pallas_call x1, Pallas kernels, on_device(): pl.pallas_call(functools.partial(distance_kernel, batches, starts, count)...  7.93 us
    pallas_call x1, Pallas kernels, on_device(): pl.pallas_call(functools.partial(gradient_kernel, place, count), out_shap...  6.39 us
    all_to_all x1, starting transfers between devices, on_device(): lax.all_to_all(members.transpose(2, 0, 1, 3, 4), 'member', 0, 0, tiled=True)  5.76 us
    reshape x2, local copies, waits for them, and re-layouts, on_device(): back.reshape(groups, local, lines, parts, slots)  4.57 us
  transfers between devices with their start and end apart: 2, of which 2 were waited for; matrix products, arithmetic and copies ran while one was open for 1% of the time, Pallas kernels for 1%

profile of v1, /device:TPU:8, one launch (start us, length us, event | category | flops | bytes accessed | tf_op | source)
XLA Modules:
  0.0 104.0 jit_solution(9483630117195893654)
XLA Ops:
  0.0 0.0 copy-start
  0.0 0.0 copy-start.2
  0.0 0.0 copy-start.1
  0.0 3.1 %copy.19 = bf16[4,12,8,2,768]{4,3,1,0,2:T(2,128)(2,1)} copy(bf16[4,12,8,2,768]{4,3,2,1,0:T(2,128)(2,1)} %param.5) | data formatting | bytes 2359296 | tf_op args[0]
  3.1 5.8 %all-to-all-start = ((bf16[8,4,12,2,768]{4,3,2,1,0:T(2,128)(2,1)}), bf16[8,4,12,2,768]{4,3,2,1,0:T(2,128)(2,1)S(1)}, u32[]{:S(2)}, u32[]{:S(2)}) async-start(bf16[8,4,12,2,768]{4,3,2,1,0:T(2,128)(2,1)} %bitcast.16), calls=%async_computation | async-start | bytes 2359296 | tf_op jit(solution)/shard_map/all_to_all | solution.py:178
  8.9 0.0 copy-done.2
  8.9 0.0 copy-done.1
  8.9 0.8 slot_weights.1.w_ref
  9.7 0.0 copy-done
  9.8 14.8 %all-to-all-done = bf16[8,4,12,2,768]{4,3,2,1,0:T(2,128)(2,1)S(1)} async-done(((bf16[8,4,12,2,768]{4,3,2,1,0:T(2,128)(2,1)}), bf16[8,4,12,2,768]{4,3,2,1,0:T(2,128)(2,1)S(1)}, u32[]{:S(2)}, u32[]{:S(2)}) %all-to-all-start) | async-done | bytes 1179680 | tf_op jit(solution)/shard_map/all_to_all | solution.py:178
  24.6 0.8 reshape.21
  25.4 0.0 copy-start.3
  25.4 1.2 %copy.12 = bf16[32,12,6,2,128]{4,3,2,1,0:T(2,128)(2,1)S(1)} copy(bf16[32,12,6,2,128]{4,2,3,1,0:T(8,128)(2,1)S(1)} %bitcast.24) | data formatting | bytes 2359296 | tf_op jit(solution)/shard_map/transpose | solution.py:179
  26.6 7.9 %distances.1 = f32[8,128]{1,0:T(8,128)S(1)} custom-call(bf16[32,144,128]{2,1,0:T(8,128)(2,1)S(1)} %bitcast.17, bf16[144,128]{1,0:T(8,128)(2,1)S(1)} %bitcast.20, f32[144,128]{1,0:T(8,128)S(1)} %slot_weights.1.w_ref), custom_call_target="tpu_custom_call" | custom-call | tf_op jit(solution)/shard_map/distances/pallas_call | solution.py:184
  34.5 0.7 broadcast_in_dim.5
  35.2 10.6 %all-to-all-start.1 = ((f32[32,8,128]{2,1,0:T(8,128)}), f32[32,8,128]{2,1,0:T(8,128)S(1)}, u32[]{:S(2)}, u32[]{:S(2)}) async-start(f32[32,8,128]{2,1,0:T(8,128)} %broadcast_in_dim.5), calls=%async_computation.1 | async-start | bytes 262144 | tf_op jit(solution)/shard_map/all_to_all | solution.py:194
  45.8 0.0 copy-done.3
  45.8 0.6 dynamic_slice.8
  47.0 10.8 %all-to-all-done.1.got_ref = f32[32,8,128]{2,1,0:T(8,128)S(1)} async-done(((f32[32,8,128]{2,1,0:T(8,128)}), f32[32,8,128]{2,1,0:T(8,128)S(1)}, u32[]{:S(2)}, u32[]{:S(2)}) %all-to-all-start.1) | async-done | bytes 131104 | tf_op jit(solution)/shard_map/all_to_all | solution.py:194
  57.8 6.4 %gradients.1 = f32[32,144,128]{2,1,0:T(8,128)S(1)} custom-call(f32[32,8,128]{2,1,0:T(8,128)S(1)} %all-to-all-done.1.got_ref, bf16[32,144,128]{2,1,0:T(8,128)(2,1)S(1)} %bitcast.18, bf16[144,128]{1,0:T(8,128)(2,1)S(1)} %bitcast.21, f32[144,128]{1,0:T(8,128)S(1)} %slot_weights.1.w_ref, f32[1]{0:T(128)S(6)} %mul.3.c_ref), custom_call_target="tpu_custom_call" | custom-call | tf_op jit(solution)/shard_map/gradients/pallas_call | solution.py:198
  64.2 0.4 copy.18
  64.6 1.7 %reshape.26 = f32[8,4,12,2,768]{4,0,3,2,1:T(8,128)} reshape(f32[8,4,12,2,6,128]{5,4,0,3,2,1:T(8,128)S(1)} %bitcast.22) | data formatting | bytes 4718592 | tf_op jit(solution)/shard_map/reshape | solution.py:212
  66.3 2.9 %copy.14 = f32[8,4,12,2,768]{4,3,2,1,0:T(2,128)S(1)} copy(f32[8,4,12,2,768]{4,0,3,2,1:T(8,128)} %reshape.26) | data formatting | bytes 4718592 | tf_op jit(solution)/shard_map/reshape | solution.py:212
  69.2 32.1 %all_to_all.15 = f32[8,4,12,2,768]{4,3,2,1,0:T(2,128)S(1)} all-to-all(f32[8,4,12,2,768]{4,3,2,1,0:T(2,128)S(1)} %copy.14), channel_id=1, replica_groups=mesh['order'=32,'member'=8] {'member'}, dimensions={0} | all-to-all | bytes 4718592 | tf_op jit(solution)/shard_map/all_to_all | solution.py:212
  101.3 2.7 %copy.15 = f32[4,12,8,2,768]{4,3,2,1,0:T(2,128)} copy(f32[4,12,8,2,768]{4,3,1,0,2:T(2,128)S(1)} %bitcast.23) | data formatting | bytes 4718592 | tf_op jit(solution)/shard_map/transpose | solution.py:213
  (3 shorter events, 0.0 us)
Async XLA Ops:
  0.0 9.7 %copy-start = (bf16[12,8,2,768]{3,2,1,0:T(2,128)(2,1)S(1)}, bf16[12,8,2,768]{3,2,1,0:T(2,128)(2,1)}, u32[]{:S(2)}) copy-start(bf16[12,8,2,768]{3,2,1,0:T(2,128)(2,1)} %param.6) | copy-start | bytes 884740
  0.0 8.9 %copy-start.2 = (f32[721]{0:T(1024)S(1)}, f32[721]{0:T(1024)}, u32[]{:S(2)}) copy-start(f32[721]{0:T(1024)} %param.8) | copy-start | bytes 8656
  0.0 8.9 %copy-start.1 = (s32[12]{0:T(128)S(1)}, s32[12]{0:T(128)}, u32[]{:S(2)}) copy-start(s32[12]{0:T(128)} %order_ref.1) | copy-start | bytes 148
  3.1 21.4 %all-to-all-start = ((bf16[8,4,12,2,768]{4,3,2,1,0:T(2,128)(2,1)}), bf16[8,4,12,2,768]{4,3,2,1,0:T(2,128)(2,1)S(1)}, u32[]{:S(2)}, u32[]{:S(2)}) async-start(bf16[8,4,12,2,768]{4,3,2,1,0:T(2,128)(2,1)} %bitcast.16), calls=%async_computation | async-start | bytes 2359296 | tf_op jit(solution)/shard_map/all_to_all | solution.py:178
  25.4 20.4 %copy-start.3 = (f32[8]{0:T(128)S(1)}, f32[8]{0:T(128)}, u32[]{:S(2)}) copy-start(f32[8]{0:T(128)} %param.9) | copy-start | bytes 100
  35.2 22.6 %all-to-all-start.1 = ((f32[32,8,128]{2,1,0:T(8,128)}), f32[32,8,128]{2,1,0:T(8,128)S(1)}, u32[]{:S(2)}, u32[]{:S(2)}) async-start(f32[32,8,128]{2,1,0:T(8,128)} %broadcast_in_dim.5), calls=%async_computation.1 | async-start | bytes 262144 | tf_op jit(solution)/shard_map/all_to_all | solution.py:194

commit v2 on v1

v2 whole, which is shorter than its diff:
```python
import functools

import jax
import jax.numpy as jnp
from jax import lax
from jax.experimental import pallas as pl
from jax.experimental.layout import Layout, with_layout_constraint
from jax.experimental.pallas import tpu as pltpu
from jax.sharding import PartitionSpec as P

epsilon = 1e-06
LANES = 128
GROUP = 4
BATCH = 32
POWER = 13.0


def pair_table(stages, local, count):
    members_of = [list(range(g * local, (g + 1) * local)) for g in range(count // local)]
    plans, place, start = [], {}, 0
    for stage in stages:
        cross = [(a, b) for b in stage for a in range(b)]
        lists = [
            [(m, n) for a, b in cross[at : at + 2] for m in members_of[a] for n in members_of[b]]
            for at in range(0, len(cross), 2)
        ]
        for at in range(0, len(stage), 2):
            own = [members_of[g] for g in stage[at : at + 2]]
            inner = [(m, n) for g in own for i, m in enumerate(g) for n in g[i + 1 :]]
            lists.append(inner + [(m, count) for g in own for m in g])
        if len(lists) > 1 and len(lists[-1]) + len(lists[-2]) <= BATCH:
            lists[-2:] = [lists[-2] + lists[-1]]
        plan, first = [], start
        for batch in lists:
            plan.append((batch, start - first))
            for index, pair in enumerate(batch):
                place[pair] = start + index
            start += -(-len(batch) // 8) * 8
        start = -(-start // LANES) * LANES
        plans.append((plan, (start - first) // LANES))
    return plans, place, start


def fold_rows(blocks):
    row = lax.broadcasted_iota(jnp.int32, (8, LANES), 0)
    for half in (4, 2, 1):
        low = (row & half) == 0
        count = len(blocks) // 2
        merged = []
        for i in range(count):
            a, b = blocks[i], blocks[i + count]
            kept = jnp.where(low, a, b)
            moved = jnp.where(low, b, a)
            merged.append(kept + (pltpu.roll(moved, half, 0) if half == 4 else swap(moved, half, low)))
        blocks = merged
    return blocks[0]


def swap(block, half, low):
    return jnp.where(low, pltpu.roll(block, 8 - half, 0), pltpu.roll(block, half, 0))


def prepare_kernel(degrees, shifts, x_ref, y_ref, order_from, table_from, c_from, *refs):
    *out_refs, target_ref, weight_ref, drawn_ref, near_ref, order_ref, table_ref, c_ref, in_sems, out_sems, sems = refs
    local = near_ref.shape[0]
    me = lax.axis_index("member")
    into = [pltpu.make_async_copy(x_ref.at[m], near_ref.at[m], in_sems.at[m]) for m in range(local)]
    small = [
        pltpu.make_async_copy(order_from, order_ref, sems.at[0]),
        pltpu.make_async_copy(table_from, table_ref, sems.at[1]),
        pltpu.make_async_copy(c_from, c_ref, sems.at[2]),
        pltpu.make_async_copy(y_ref.at[:, me], target_ref, sems.at[3]),
    ]
    for copy in into + small:
        copy.start()
    out = []
    for m in range(local):
        into[m].wait()
        for step, shift in enumerate(shifts):
            channel = jnp.bitwise_xor(me, shift)
            copy = pltpu.make_async_copy(near_ref.at[m, :, channel], out_refs[step].at[m], out_sems.at[m, step])
            copy.start()
            out.append(copy)
    for copy in small:
        copy.wait()

    parts = target_ref.shape[-1] // LANES
    slots = parts * LANES
    line = table_ref[...].reshape(1, degrees)
    line = jnp.concatenate([line, jnp.zeros((1, slots - degrees), jnp.float32)], axis=1)
    table = jnp.broadcast_to(line, (8, slots))
    slot = lax.broadcasted_iota(jnp.int32, table.shape, 1)
    tail = pltpu.roll(table, 1, 1)
    half = 0.5 * c_ref[me]
    for row in range(order_ref.shape[0]):
        order = order_ref[row]
        head = pltpu.roll(table, lax.rem(slots - jnp.maximum(order, 0), slots), 1)
        leading = slot < degrees - order
        second = (slot <= degrees) & (2 * order < degrees - 1)
        usable = (order >= 0) & (leading | second)
        times = jnp.where(leading & (order == 0), 1.0, 2.0)
        line = jnp.where(usable, jnp.where(leading, head, tail) * times, 0.0)
        for part in range(parts):
            at = (row * parts + part) * 2
            piece = line[0:2, part * LANES : (part + 1) * LANES]
            weight_ref[at : at + 2, :] = piece
            drawn_ref[at : at + 2, :] = piece * half
    for copy in out:
        copy.wait()


def distance_kernel(plan, blocks, fresh, earlier, with_target, last, *refs):
    refs = list(refs)
    old_refs = [refs.pop(0) for _ in range(blocks)]
    new_refs = [refs.pop(0) for _ in range(fresh)]
    y_ref, w_ref = refs.pop(0), refs.pop(0)
    before = [refs.pop(0) for _ in range(earlier)]
    line_ref = refs.pop(0)
    scaled_refs = [refs.pop(0) for _ in range(fresh)]
    target_ref = refs.pop(0) if with_target else y_ref
    sums_ref = refs.pop(0)
    rows = w_ref.shape[0]
    local = new_refs[0].shape[0]

    def scale(i, carry):
        at = pl.ds(pl.multiple_of(i * 16, 16), 16)
        root = jnp.sqrt(w_ref[at, :])
        for x_ref, scaled_ref in zip(new_refs, scaled_refs):
            for m in range(local):
                scaled_ref[m, at, :] = x_ref[m, at, :].astype(jnp.float32) * root
        if with_target:
            target_ref[at, :] = y_ref[at, :].astype(jnp.float32) * root
        return carry

    lax.fori_loop(0, rows // 16, scale, 0)
    every = old_refs + scaled_refs

    def piece(m, at):
        if m // local < blocks + fresh:
            return every[m // local][m % local, at : at + 8, :]
        return target_ref[at : at + 8, :]

    zero = jnp.zeros((8, LANES), jnp.float32)
    sums_ref[...] = jnp.zeros_like(sums_ref)
    for batch, start in plan:
        used = sorted({m for pair in batch for m in pair})
        sums = [zero] * len(batch)
        for at in range(0, rows, 8):
            held = {m: piece(m, at) for m in used}
            for index, (m, n) in enumerate(batch):
                difference = held[m] - held[n]
                sums[index] = sums[index] + difference * difference
        sums += [zero] * (-len(sums) % 8)
        for at in range(0, len(sums), 8):
            sums_ref[start + at : start + at + 8, :] = fold_rows(sums[at : at + 8])
    to = 0
    if last:
        line_ref[...] = jnp.zeros_like(line_ref)
        for ref in before:
            line_ref[to : to + ref.shape[0], :] = ref[...]
            to += ref.shape[0]
    for block in range(sums_ref.shape[0] // LANES):
        square = sums_ref[block * LANES : (block + 1) * LANES, :].T
        line_ref[to + block : to + block + 1, :] = jnp.sum(square, axis=0, keepdims=True)


def gradient_kernel(place, count, shifts, got_ref, *refs):
    *x_refs, y_ref, w_ref, out_ref, table_ref, wide_ref, pull_ref = refs
    rows = w_ref.shape[0]
    groups = out_ref.shape[0]
    local = count // groups
    slot = [jnp.bitwise_xor(lax.axis_index("member"), shift) for shift in shifts]
    squares = jnp.sum(got_ref[...], axis=0)
    inverse = lax.rsqrt(squares + epsilon)
    largest = jnp.max(squares * inverse * inverse, axis=(0, 1), keepdims=True)
    power = POWER + jnp.floor(jnp.clip(-0.5 * jnp.log2(jnp.maximum(largest, 1e-30)), 0.0, 50.0))
    scale = jnp.broadcast_to(jnp.exp2(power), (16, LANES))
    for group in range(out_ref.shape[0]):
        out_ref[group, local * rows :, :] = jnp.broadcast_to(power, (16, LANES))
    columns = inverse.T
    for block in range(table_ref.shape[0] // LANES):
        column = jnp.broadcast_to(columns[:, block : block + 1], (LANES, LANES))
        table_ref[block * LANES : (block + 1) * LANES, :] = column

    def entry(m, n):
        at = place[(min(m, n), max(m, n))]
        return jnp.broadcast_to(table_ref[at : at + 1, :], (16, LANES))

    def slab(i, carry):
        at = pl.ds(pl.multiple_of(i * 16, 16), 16)
        for m in range(count):
            wide_ref[m] = x_refs[m // local][m % local, at, :].astype(jnp.float32)
        target = y_ref[at, :].astype(jnp.float32)
        weight = w_ref[at, :] * scale
        share = 1.0 / (count - 1)
        for first in range(0, count, GROUP):
            own = list(range(first, first + GROUP))
            held = [wide_ref[m] for m in own]
            if first == 0:
                pulls = [jnp.zeros((16, LANES), jnp.float32) for _ in own]
            else:
                pulls = [pull_ref[m] for m in own]
            for i_m in range(GROUP):
                for i_n in range(i_m + 1, GROUP):
                    term = entry(own[i_m], own[i_n]) * (held[i_m] - held[i_n])
                    pulls[i_m] += term
                    pulls[i_n] -= term
            for second in range(first + GROUP, count, GROUP):
                for n in range(second, second + GROUP):
                    partner = wide_ref[n]
                    back = jnp.zeros((16, LANES), jnp.float32) if first == 0 else pull_ref[n]
                    for i_m in range(GROUP):
                        term = entry(own[i_m], n) * (held[i_m] - partner)
                        pulls[i_m] += term
                        back -= term
                    pull_ref[n] = back
            for i_m in range(GROUP):
                toward = (held[i_m] - target) * entry(own[i_m], count)
                there = pl.ds(pl.multiple_of(own[i_m] % local * rows + i * 16, 16), 16)
                out_ref[slot[own[i_m] // local], there, :] = weight * (toward - pulls[i_m] * share)
        return carry

    lax.fori_loop(0, rows // 16, slab, 0)


def restore_kernel(degrees, lines, x_ref, out_ref, held_ref, sems):
    local, each, _ = held_ref.shape
    channels = x_ref.shape[0]
    rows = each // channels
    run = rows // lines
    copies = []
    for m in range(local):
        for c in range(channels):
            factor = jnp.exp2(-x_ref[c, local * rows : local * rows + 1, :]) * (2.0 * degrees)
            for line in range(lines):
                at = m * rows + line * run
                to = (line * channels + c) * run
                held_ref[m, to : to + run, :] = x_ref[c, at : at + run, :] * factor
        copy = pltpu.make_async_copy(held_ref.at[m], out_ref.at[pl.ds(m * each, each)], sems.at[m])
        copy.start()
        copies.append(copy)
    for copy in copies:
        copy.wait()


def on_device(members, observed, pair_order, degree_weight, cotangent):
    groups = lax.axis_size("member")
    spread = lax.axis_size("order")
    local, lines, channels, parts, slots = members.shape
    count = local * groups
    tiles = slots // LANES
    rows = lines * parts * tiles
    degrees = degree_weight.shape[0]
    shifts = (0, 4, 6, 2, 5, 7, 1, 3)
    stages = [[0, 1, 2], [3], [4], [5, 6], [7]]
    plans, place, entries = pair_table(stages, local, count)
    vmem = pltpu.CompilerParams(vmem_limit_bytes=16 << 20)
    whole = pl.BlockSpec(memory_space=pltpu.VMEM)
    outside = pl.BlockSpec(memory_space=pltpu.HBM)

    surface = jax.ShapeDtypeStruct((rows, LANES), jnp.float32)
    *sent, target, weights, drawn = pl.pallas_call(
        functools.partial(prepare_kernel, degrees, shifts),
        out_shape=(jax.ShapeDtypeStruct((local, lines, parts, slots), members.dtype),) * channels
        + (jax.ShapeDtypeStruct((lines, parts, slots), observed.dtype), surface, surface),
        in_specs=[outside] * 5,
        out_specs=(whole,) * (channels + 3),
        scratch_shapes=[
            pltpu.VMEM((local, lines, channels, parts, slots), members.dtype),
            pltpu.SMEM(pair_order.shape, jnp.int32),
            pltpu.VMEM(degree_weight.shape, jnp.float32),
            pltpu.SMEM(cotangent.shape, jnp.float32),
            pltpu.SemaphoreType.DMA((local,)),
            pltpu.SemaphoreType.DMA((local, channels)),
            pltpu.SemaphoreType.DMA((4,)),
        ],
        compiler_params=vmem,
        name="prepare",
    )(*(pltpu.with_memory_space_constraint(x, pltpu.HBM) for x in (members, observed, pair_order, degree_weight, cotangent)))
    target = as_rows(target).reshape(rows, LANES)
    held = [as_rows(sent[0]).reshape(local, rows, LANES)]
    for step in range(1, groups):
        block = sent[step]
        if step > 5:
            block, held[1] = lax.optimization_barrier((block, held[1]))
        block = lax.ppermute(block, "member", [(i, i ^ shifts[step]) for i in range(groups)])
        held.append(as_rows(block).reshape(local, rows, LANES))

    scaled, sums, against = [], [], target
    for stage, (plan, height) in zip(stages, plans):
        first, last = stage is stages[0], stage is stages[-1]
        fresh = [held[g] for g in stage]
        before = sums if last else []
        block = jax.ShapeDtypeStruct((local, rows, LANES), jnp.float32)
        lead = jax.ShapeDtypeStruct((8 if last else height, LANES), jnp.float32)
        result = pl.pallas_call(
            functools.partial(distance_kernel, plan, len(scaled), len(fresh), len(before), first, last),
            out_shape=(lead,) + (block,) * len(fresh) + ((surface,) if first else ()),
            scratch_shapes=[pltpu.VMEM((height * LANES, LANES), jnp.float32)],
            compiler_params=vmem,
            name="distances",
        )(*scaled, *fresh, against, weights, *before)
        sums = sums + [result[0]]
        scaled = scaled + list(result[1 : 1 + len(fresh)])
        if first:
            against = result[-1]
    got = lax.all_to_all(jnp.broadcast_to(sums[-1][None], (spread, 8, LANES)), "order", 0, 0, tiled=True)

    gradient = pl.pallas_call(
        functools.partial(gradient_kernel, place, count, shifts),
        out_shape=jax.ShapeDtypeStruct((groups, local * rows + 16, LANES), jnp.float32),
        scratch_shapes=[
            pltpu.VMEM((entries, LANES), jnp.float32),
            pltpu.VMEM((count, 16, LANES), jnp.float32),
            pltpu.VMEM((count, 16, LANES), jnp.float32),
        ],
        compiler_params=vmem,
        name="gradients",
    )(got, *held, target, drawn)

    back = lax.all_to_all(gradient.astype(jnp.float16), "member", 0, 0, tiled=True).astype(jnp.float32)
    back = pl.pallas_call(
        functools.partial(restore_kernel, degrees, lines),
        out_shape=jax.ShapeDtypeStruct((local * rows * channels, LANES), jnp.float32),
        in_specs=[whole],
        out_specs=outside,
        scratch_shapes=[
            pltpu.VMEM((local, rows * channels, LANES), jnp.float32),
            pltpu.SemaphoreType.DMA((local,)),
        ],
        compiler_params=vmem,
        name="restore",
    )(back)
    return from_rows(back.reshape(local * lines * channels, tiles, parts, LANES)).reshape(members.shape)


def as_rows(block):
    parts, slots = block.shape[-2:]
    split = block.reshape(-1, parts, slots // LANES, LANES)
    return with_layout_constraint(split, Layout((0, 2, 1, 3))).transpose(0, 2, 1, 3)


def from_rows(block):
    count, tiles, parts, lanes = block.shape
    split = with_layout_constraint(block.transpose(0, 2, 1, 3), Layout((0, 2, 1, 3)))
    return split.reshape(count, parts, tiles * lanes)


def solution(mesh):
    placed = (
        P("member", "order", None, None, None),
        P("order", None, None, None),
        P("order"),
        P(),
        P(),
    )
    return jax.shard_map(
        on_device,
        mesh=mesh,
        in_specs=placed,
        out_specs=P("member", "order", None, None, None),
        check_vma=False,
    )
```

time: 105 us -> 73.4 us (0.70)
  waiting for transfers between devices: 25.6 us -> 4.58 us
  local copies, waits for them, and re-layouts: 14.2 us -> 0.01 us
  blocking collectives: 32.1 us -> 42.2 us
  starting transfers between devices: 16.3 us -> 11.1 us
    all_to_all x2 -> x0, waiting for transfers between devices: 25.6 us -> none  [the longest x1 14.8 us: on_device(): lax.all_to_all(members.transpose(2, 0, 1, 3, 4), 'member', 0, 0, tiled=True)]
    all_to_all x2 -> x0, starting transfers between devices: 16.3 us -> none  [the longest x1 10.6 us: on_device(): lax.all_to_all(jnp.broadcast_to(sums[None], (spread, 8, LANES)), 'order',...]
    ppermute x0 -> x7, starting transfers between devices: none -> 11.1 us  [on_device(): lax.ppermute(block, 'member', [(i, i ^ shifts[step]) for i in range(group...]
    all_to_all x1 -> x2, blocking collectives: 32.1 us -> 42.2 us  [the longest x1 22.3 us: on_device(): lax.all_to_all(jnp.broadcast_to(sums[-1][None], (spread, 8, LANES)), 'ord...]
    reshape x4 -> x0, local copies, waits for them, and re-layouts: 5.81 us -> none  [the longest x2 4.57 us: on_device(): back.reshape(groups, local, lines, parts, slots)]
    ppermute x0 -> x7, waiting for transfers between devices: none -> 4.58 us  [on_device(): lax.ppermute(block, 'member', [(i, i ^ shifts[step]) for i in range(group...]
    transpose x2 -> x0, local copies, waits for them, and re-layouts: 3.95 us -> none  [the longest x1 2.73 us: on_device(): return back.transpose(1, 2, 0, 3, 4)]
    unnamed x9 -> x0, local copies, waits for them, and re-layouts: 3.16 us -> none
  transfers between devices with their start and end apart: 2 -> 7, of which waited for: 2 -> 3; matrix products, arithmetic and copies ran while one was open for 1% -> 0% of each run, Pallas kernels for 1% -> 5%
where the time goes in v2:
time: 73.4 us; the launch traced here: 72.8 us
  blocking collectives  42.2 us (57%)
  Pallas kernels  14.5 us (20%)
  starting transfers between devices  11.1 us (15%)
  waiting for transfers between devices  4.58 us (6%)
    all_to_all x1, blocking collectives, on_device(): lax.all_to_all(jnp.broadcast_to(sums[-1][None], (spread, 8, LANES)), 'ord...  22.3 us
    all_to_all x1, blocking collectives, on_device(): lax.all_to_all(gradient.astype(jnp.float16), 'member', 0, 0, tiled=True)  19.9 us
    ppermute x7, starting transfers between devices, on_device(): lax.ppermute(block, 'member', [(i, i ^ shifts[step]) for i in range(group...  11.1 us
    pallas_call x1, Pallas kernels, on_device(): pl.pallas_call(functools.partial(gradient_kernel, place, count, shifts),...  5.85 us
    pallas_call x5, Pallas kernels, on_device(): pl.pallas_call(functools.partial(distance_kernel, plan, len(scaled), len(...  5.23 us
    ppermute x7, waiting for transfers between devices, on_device(): lax.ppermute(block, 'member', [(i, i ^ shifts[step]) for i in range(group...  4.58 us
    pallas_call x1, Pallas kernels, on_device(): pl.pallas_call(functools.partial(prepare_kernel, degrees, shifts), out_sh...  1.97 us
    pallas_call x1, Pallas kernels, on_device(): pl.pallas_call(functools.partial(restore_kernel, degrees, lines), out_sha...  1.49 us
  transfers between devices with their start and end apart: 7, of which 3 were waited for; matrix products, arithmetic and copies ran while one was open for 0% of the time, Pallas kernels for 5%

profile of v2, /device:TPU:8, one launch (start us, length us, event | category | flops | bytes accessed | tf_op | source)
XLA Modules:
  0.0 72.8 jit_solution(11458736557532640393)
XLA Ops:
  0.0 2.0 %prepare.1 = (bf16[4,12,2,768]{3,2,1,0:T(2,128)(2,1)S(1)}, bf16[4,12,2,768]{3,2,1,0:T(2,128)(2,1)S(1)}, bf16[4,12,2,768]{3,2,1,0:T(2,128)(2,1)S(1)}, bf16[4,12,2...) custom-call(bf16[4,12,8,2,768]{4,3,2,1,0:T(2,128)(2,1)} %x_ref.1, ...), custom_call_target="tpu_custom_call" | custom-call | tf_op jit(solution)/shard_map/prepare/pallas_call | solution.py:262
  2.0 2.3 %collective-permute-start = (bf16[4,12,2,768]{3,2,1,0:T(2,128)(2,1)S(1)}, bf16[4,12,2,768]{3,2,1,0:T(2,128)(2,1)S(1)}, u32[]{:S(2)}, u32[]{:S(2)}) collective-permute-start(bf16[4,12,2,768]{3,2,1,0:T(2,128)(2,1)S(1)} %get-tuple-element.36), channel_id=1, source_target_pairs={{0,4},{1,5},{2,6},{3,7},{4,0},{5,1},{6,2},{7,3},{8,12},{9,13},{10,... | collective-permute-start | bytes 442376 | tf_op jit(solution)/shard_map/ppermute | solution.py:286
  4.2 2.3 %collective-permute-start.1 = (bf16[4,12,2,768]{3,2,1,0:T(2,128)(2,1)S(1)}, bf16[4,12,2,768]{3,2,1,0:T(2,128)(2,1)S(1)}, u32[]{:S(2)}, u32[]{:S(2)}) collective-permute-start(bf16[4,12,2,768]{3,2,1,0:T(2,128)(2,1)S(1)} %get-tuple-element.39), channel_id=1, source_target_pairs={{0,6},{1,7},{2,4},{3,5},{4,2},{5,3},{6,0},{7,1},{8,14},{9,15},{10,... | collective-permute-start | bytes 442376 | tf_op jit(solution)/shard_map/ppermute | solution.py:286
  6.5 0.8 %collective-permute-start.2 = (bf16[4,12,2,768]{3,2,1,0:T(2,128)(2,1)S(1)}, bf16[4,12,2,768]{3,2,1,0:T(2,128)(2,1)S(1)}, u32[]{:S(2)}, u32[]{:S(2)}) collective-permute-start(bf16[4,12,2,768]{3,2,1,0:T(2,128)(2,1)S(1)} %get-tuple-element.45), channel_id=1, source_target_pairs={{0,2},{1,3},{2,0},{3,1},{4,6},{5,7},{6,4},{7,5},{8,10},{9,11},{10,... | collective-permute-start | bytes 442376 | tf_op jit(solution)/shard_map/ppermute | solution.py:286
  7.3 1.1 %collective-permute-start.3 = (bf16[4,12,2,768]{3,2,1,0:T(2,128)(2,1)S(1)}, bf16[4,12,2,768]{3,2,1,0:T(2,128)(2,1)S(1)}, u32[]{:S(2)}, u32[]{:S(2)}) collective-permute-start(bf16[4,12,2,768]{3,2,1,0:T(2,128)(2,1)S(1)} %get-tuple-element.48), channel_id=1, source_target_pairs={{0,5},{1,4},{2,7},{3,6},{4,1},{5,0},{6,3},{7,2},{8,13},{9,12},{10,... | collective-permute-start | bytes 442376 | tf_op jit(solution)/shard_map/ppermute | solution.py:286
  8.4 3.1 %collective-permute-start.4 = (bf16[4,12,2,768]{3,2,1,0:T(2,128)(2,1)S(1)}, bf16[4,12,2,768]{3,2,1,0:T(2,128)(2,1)S(1)}, u32[]{:S(2)}, u32[]{:S(2)}) collective-permute-start(bf16[4,12,2,768]{3,2,1,0:T(2,128)(2,1)S(1)} %get-tuple-element.50), channel_id=1, source_target_pairs={{0,7},{1,6},{2,5},{3,4},{4,3},{5,2},{6,1},{7,0},{8,15},{9,14},{10,... | collective-permute-start | bytes 442376 | tf_op jit(solution)/shard_map/ppermute | solution.py:286
  11.5 0.0 collective-permute-done
  11.5 0.6 collective-permute-start.5
  12.1 1.5 %collective-permute-done.1 = bf16[4,12,2,768]{3,2,1,0:T(2,128)(2,1)S(1)} collective-permute-done((bf16[4,12,2,768]{3,2,1,0:T(2,128)(2,1)S(1)}, bf16[4,12,2,768]{3,2,1,0:T(2,128)(2,1)S(1)}, u32[]{:S(2)}, u32[]{:S(2)}) %collective-permute-start.1) | collective-permute-done | bytes 147488 | tf_op jit(solution)/shard_map/ppermute | solution.py:286
  13.6 0.9 %collective-permute-start.6 = (bf16[4,12,2,768]{3,2,1,0:T(2,128)(2,1)S(1)}, bf16[4,12,2,768]{3,2,1,0:T(2,128)(2,1)S(1)}, u32[]{:S(2)}, u32[]{:S(2)}) collective-permute-start(bf16[4,12,2,768]{3,2,1,0:T(2,128)(2,1)S(1)} %get-tuple-element.54), channel_id=1, source_target_pairs={{0,3},{1,2},{2,1},{3,0},{4,7},{5,6},{6,5},{7,4},{8,11},{9,10},{10,... | collective-permute-start | bytes 442376 | tf_op jit(solution)/shard_map/ppermute | solution.py:286
  14.5 0.8 %distances.5 = (f32[1,128]{1,0:T(1,128)S(1)}, f32[4,144,128]{2,1,0:T(8,128)S(1)}, f32[4,144,128]{2,1,0:T(8,128)S(1)}, f32[4,144,128]{2,1,0:T(8,128)S(1)}, f32[144,128]{1,0:T(8,128)S(1)}) custom-call(bf16[4,144,128]{2,1,0:T(8,128)(2,1)S(1)} %bitcast.56, bf16[4,144,128]{2,1,0:T(8,128)(2,1)S(1)} %bitcast.58, bf16[4,144,128]{2,1,0:T(8,128)(2,1)S(1)} %bitcast.60, ...), custom_call_target="tpu_custom_call" | custom-call | tf_op jit(solution)/shard_map/distances/pallas_call | solution.py:296
  15.3 0.0 collective-permute-done.2
  15.4 0.7 distances.6
  16.0 2.7 %collective-permute-done.3 = bf16[4,12,2,768]{3,2,1,0:T(2,128)(2,1)S(1)} collective-permute-done((bf16[4,12,2,768]{3,2,1,0:T(2,128)(2,1)S(1)}, bf16[4,12,2,768]{3,2,1,0:T(2,128)(2,1)S(1)}, u32[]{:S(2)}, u32[]{:S(2)}) %collective-permute-start.3) | collective-permute-done | bytes 147488 | tf_op jit(solution)/shard_map/ppermute | solution.py:286
  18.8 0.8 %distances.7 = (f32[1,128]{1,0:T(1,128)S(1)}, f32[4,144,128]{2,1,0:T(8,128)S(1)}) custom-call(f32[4,144,128]{2,1,0:T(8,128)S(1)} %get-tuple-element.42.refs_0_, f32[4,144,128]{2,1,0:T(8,128)S(1)} %get-tuple-element.43.refs_1_, f32[4,144,128]{2,1,0:T(8,128)S(1)} %get-tuple-element.44.refs_2_, f32[4,144,128]{2,1,0:T(8,128)S(1)} %get-tuple-element.47.refs_3_, ...), custom_call_target="tpu_custom_call" | custom-call | tf_op jit(solution)/shard_map/distances/pallas_call | solution.py:296
  19.5 0.0 collective-permute-done.4
  19.5 0.4 collective-permute-done.5
  19.9 1.7 %distances.8 = (f32[2,128]{1,0:T(2,128)S(1)}, f32[4,144,128]{2,1,0:T(8,128)S(1)}, f32[4,144,128]{2,1,0:T(8,128)S(1)}) custom-call(f32[4,144,128]{2,1,0:T(8,128)S(1)} %get-tuple-element.42.refs_0_, f32[4,144,128]{2,1,0:T(8,128)S(1)} %get-tuple-element.43.refs_1_, f32[4,144,128]{2,1,0:T(8,128)S(1)} %get-tuple-element.44.refs_2_, ...), custom_call_target="tpu_custom_call" | custom-call | tf_op jit(solution)/shard_map/distances/pallas_call | solution.py:296
  21.6 0.0 collective-permute-done.6
  21.6 1.3 %distances.9 = (f32[8,128]{1,0:T(8,128)S(1)}, f32[4,144,128]{2,1,0:T(8,128)}) custom-call(f32[4,144,128]{2,1,0:T(8,128)S(1)} %get-tuple-element.42.refs_0_, f32[4,144,128]{2,1,0:T(8,128)S(1)} %get-tuple-element.43.refs_1_, f32[4,144,128]{2,1,0:T(8,128)S(1)} %get-tuple-element.44.refs_2_, f32[4,144,128]{2,1,0:T(8,128)S(1)} %get-tuple-element.47.refs_3_, ...), custom_call_target="tpu_custom_call" | custom-call | tf_op jit(solution)/shard_map/distances/pallas_call | solution.py:296
  22.9 22.3 %all_to_all.10.got_ref = f32[32,8,128]{2,1,0:T(8,128)S(1)} all-to-all(f32[32,8,128]{2,1,0:T(8,128)S(1)} %broadcast_in_dim.2), channel_id=1, replica_groups=mesh['order'=32,'member'=8] {'order'}, dimensions={0} | all-to-all | bytes 262144 | tf_op jit(solution)/shard_map/all_to_all | solution.py:307
  45.2 5.9 %gradients.1 = f32[8,592,128]{2,1,0:T(8,128)S(1)} custom-call(f32[32,8,128]{2,1,0:T(8,128)S(1)} %all_to_all.10.got_ref, bf16[4,144,128]{2,1,0:T(8,128)(2,1)S(1)} %bitcast.57, bf16[4,144,128]{2,1,0:T(8,128)(2,1)S(1)} %bitcast.59, bf16[4,144,128]{2,1,0:T(8,128)(2,1)S(1)} %bitcast.61, bf16[4,144,128]{2,1,0:T(8,128)(2,1)S(1)} %bitcast.51, ...), custom_call_target="tpu_custom_call" | custom-call | tf_op jit(solution)/shard_map/gradients/pallas_call | solution.py:309
  51.1 0.2 convert_element_type.6
  51.3 19.9 %all_to_all.11 = f16[8,592,128]{2,1,0:T(8,128)(2,1)S(1)} all-to-all(f16[8,592,128]{2,1,0:T(8,128)(2,1)S(1)} %convert_element_type.6), channel_id=1, replica_groups=mesh['order'=32,'member'=8] {'member'}, dimensions={0} | all-to-all | bytes 2424832 | tf_op jit(solution)/shard_map/all_to_all | solution.py:321
  71.2 0.2 convert_element_type.7.x_ref
  71.3 1.5 %restore.1 = f32[4608,128]{1,0:T(8,128)} custom-call(f32[8,592,128]{2,1,0:T(8,128)S(1)} %convert_element_type.7.x_ref), custom_call_target="tpu_custom_call" | custom-call | tf_op jit(solution)/shard_map/restore/pallas_call | solution.py:322
  (1 shorter events, 0.0 us)
Async XLA Ops:
  2.0 9.6 %collective-permute-start = (bf16[4,12,2,768]{3,2,1,0:T(2,128)(2,1)S(1)}, bf16[4,12,2,768]{3,2,1,0:T(2,128)(2,1)S(1)}, u32[]{:S(2)}, u32[]{:S(2)}) collective-permute-start(bf16[4,12,2,768]{3,2,1,0:T(2,128)(2,1)S(1)} %get-tuple-element.36), channel_id=1, source_target_pairs={{0,4},{1,5},{2,6},{3,7},{4,0},{5,1},{6,2},{7,3},{8,12},{9,13},{10,... | collective-permute-start | bytes 442376 | tf_op jit(solution)/shard_map/ppermute | solution.py:286
  4.2 9.4 %collective-permute-start.1 = (bf16[4,12,2,768]{3,2,1,0:T(2,128)(2,1)S(1)}, bf16[4,12,2,768]{3,2,1,0:T(2,128)(2,1)S(1)}, u32[]{:S(2)}, u32[]{:S(2)}) collective-permute-start(bf16[4,12,2,768]{3,2,1,0:T(2,128)(2,1)S(1)} %get-tuple-element.39), channel_id=1, source_target_pairs={{0,6},{1,7},{2,4},{3,5},{4,2},{5,3},{6,0},{7,1},{8,14},{9,15},{10,... | collective-permute-start | bytes 442376 | tf_op jit(solution)/shard_map/ppermute | solution.py:286
  6.5 8.8 %collective-permute-start.2 = (bf16[4,12,2,768]{3,2,1,0:T(2,128)(2,1)S(1)}, bf16[4,12,2,768]{3,2,1,0:T(2,128)(2,1)S(1)}, u32[]{:S(2)}, u32[]{:S(2)}) collective-permute-start(bf16[4,12,2,768]{3,2,1,0:T(2,128)(2,1)S(1)} %get-tuple-element.45), channel_id=1, source_target_pairs={{0,2},{1,3},{2,0},{3,1},{4,6},{5,7},{6,4},{7,5},{8,10},{9,11},{10,... | collective-permute-start | bytes 442376 | tf_op jit(solution)/shard_map/ppermute | solution.py:286
  7.3 11.4 %collective-permute-start.3 = (bf16[4,12,2,768]{3,2,1,0:T(2,128)(2,1)S(1)}, bf16[4,12,2,768]{3,2,1,0:T(2,128)(2,1)S(1)}, u32[]{:S(2)}, u32[]{:S(2)}) collective-permute-start(bf16[4,12,2,768]{3,2,1,0:T(2,128)(2,1)S(1)} %get-tuple-element.48), channel_id=1, source_target_pairs={{0,5},{1,4},{2,7},{3,6},{4,1},{5,0},{6,3},{7,2},{8,13},{9,12},{10,... | collective-permute-start | bytes 442376 | tf_op jit(solution)/shard_map/ppermute | solution.py:286
  8.4 11.1 %collective-permute-start.4 = (bf16[4,12,2,768]{3,2,1,0:T(2,128)(2,1)S(1)}, bf16[4,12,2,768]{3,2,1,0:T(2,128)(2,1)S(1)}, u32[]{:S(2)}, u32[]{:S(2)}) collective-permute-start(bf16[4,12,2,768]{3,2,1,0:T(2,128)(2,1)S(1)} %get-tuple-element.50), channel_id=1, source_target_pairs={{0,7},{1,6},{2,5},{3,4},{4,3},{5,2},{6,1},{7,0},{8,15},{9,14},{10,... | collective-permute-start | bytes 442376 | tf_op jit(solution)/shard_map/ppermute | solution.py:286
  11.5 8.4 %collective-permute-start.5 = (bf16[4,12,2,768]{3,2,1,0:T(2,128)(2,1)S(1)}, bf16[4,12,2,768]{3,2,1,0:T(2,128)(2,1)S(1)}, u32[]{:S(2)}, u32[]{:S(2)}) collective-permute-start(bf16[4,12,2,768]{3,2,1,0:T(2,128)(2,1)S(1)} %get-tuple-element.51), channel_id=1, source_target_pairs={{0,1},{1,0},{2,3},{3,2},{4,5},{5,4},{6,7},{7,6},{8,9},{9,8},{10,11... | collective-permute-start | bytes 442376 | tf_op jit(solution)/shard_map/ppermute | solution.py:286
  13.6 8.0 %collective-permute-start.6 = (bf16[4,12,2,768]{3,2,1,0:T(2,128)(2,1)S(1)}, bf16[4,12,2,768]{3,2,1,0:T(2,128)(2,1)S(1)}, u32[]{:S(2)}, u32[]{:S(2)}) collective-permute-start(bf16[4,12,2,768]{3,2,1,0:T(2,128)(2,1)S(1)} %get-tuple-element.54), channel_id=1, source_target_pairs={{0,3},{1,2},{2,1},{3,0},{4,7},{5,6},{6,5},{7,4},{8,11},{9,10},{10,... | collective-permute-start | bytes 442376 | tf_op jit(solution)/shard_map/ppermute | solution.py:286

commit v3 on v2

--- a/solution.py
+++ b/solution.py
@@ -164,23 +164,34 @@
         line_ref[to + block : to + block + 1, :] = jnp.sum(square, axis=0, keepdims=True)
 
 
-def gradient_kernel(place, count, shifts, got_ref, *refs):
-    *x_refs, y_ref, w_ref, out_ref, table_ref, wide_ref, pull_ref = refs
+def gradient_kernel(place, count, turn, rest, first, *refs):
+    refs = list(refs)
+    from_refs = [refs.pop(0) for _ in range(1 if first else 2)]
+    x_refs = [refs.pop(0) for _ in range(count // GROUP)]
+    y_ref, w_ref = refs.pop(0), refs.pop(0)
+    before = {} if first else {g: refs.pop(0) for g in turn}
+    out_refs = {g: refs.pop(0) for g in turn}
+    after = {g: refs.pop(0) for g in rest}
+    if first:
+        table_ref, power_ref, wide_ref, pull_ref = refs
+        squares = jnp.sum(from_refs[0][...], axis=0)
+        inverse = lax.rsqrt(squares + epsilon)
+        largest = jnp.max(squares * inverse * inverse, axis=(0, 1), keepdims=True)
+        power = POWER + jnp.floor(jnp.clip(-0.5 * jnp.log2(jnp.maximum(largest, 1e-30)), 0.0, 50.0))
+        power = jnp.broadcast_to(power, (16, LANES))
+        power_ref[...] = power
+        columns = inverse.T
+        for block in range(table_ref.shape[0] // LANES):
+            column = jnp.broadcast_to(columns[:, block : block + 1], (LANES, LANES))
+            table_ref[block * LANES : (block + 1) * LANES, :] = column
+    else:
+        wide_ref, pull_ref = refs
+        table_ref = from_refs[0]
+        power = from_refs[1][...]
     rows = w_ref.shape[0]
-    groups = out_ref.shape[0]
-    local = count // groups
-    slot = [jnp.bitwise_xor(lax.axis_index("member"), shift) for shift in shifts]
-    squares = jnp.sum(got_ref[...], axis=0)
-    inverse = lax.rsqrt(squares + epsilon)
-    largest = jnp.max(squares * inverse * inverse, axis=(0, 1), keepdims=True)
-    power = POWER + jnp.floor(jnp.clip(-0.5 * jnp.log2(jnp.maximum(largest, 1e-30)), 0.0, 50.0))
-    scale = jnp.broadcast_to(jnp.exp2(power), (16, LANES))
-    for group in range(out_ref.shape[0]):
-        out_ref[group, local * rows :, :] = jnp.broadcast_to(power, (16, LANES))
-    columns = inverse.T
-    for block in range(table_ref.shape[0] // LANES):
-        column = jnp.broadcast_to(columns[:, block : block + 1], (LANES, LANES))
-        table_ref[block * LANES : (block + 1) * LANES, :] = column
+    scale = jnp.exp2(power)
+    for g in turn:
+        out_refs[g][GROUP * rows :, :] = power
 
     def entry(m, n):
         at = place[(min(m, n), max(m, n))]
@@ -188,16 +199,21 @@
 
     def slab(i, carry):
         at = pl.ds(pl.multiple_of(i * 16, 16), 16)
-        for m in range(count):
-            wide_ref[m] = x_refs[m // local][m % local, at, :].astype(jnp.float32)
+        for g in turn + rest:
+            for k in range(GROUP):
+                wide_ref[g * GROUP + k] = x_refs[g][k, at, :].astype(jnp.float32)
         target = y_ref[at, :].astype(jnp.float32)
         weight = w_ref[at, :] * scale
         share = 1.0 / (count - 1)
-        for first in range(0, count, GROUP):
-            own = list(range(first, first + GROUP))
+        zero = jnp.zeros((16, LANES), jnp.float32)
+        fresh = {g: not before for g in turn + rest}
+        for index, g in enumerate(turn):
+            own = list(range(g * GROUP, (g + 1) * GROUP))
             held = [wide_ref[m] for m in own]
-            if first == 0:
-                pulls = [jnp.zeros((16, LANES), jnp.float32) for _ in own]
+            if fresh[g]:
+                pulls = [zero] * GROUP
+            elif index == 0:
+                pulls = [before[g][k, at, :] for k in range(GROUP)]
             else:
                 pulls = [pull_ref[m] for m in own]
             for i_m in range(GROUP):
@@ -205,37 +221,49 @@
                     term = entry(own[i_m], own[i_n]) * (held[i_m] - held[i_n])
                     pulls[i_m] += term
                     pulls[i_n] -= term
-            for second in range(first + GROUP, count, GROUP):
-                for n in range(second, second + GROUP):
+            for h in turn[index + 1 :] + rest:
+                for k in range(GROUP):
+                    n = h * GROUP + k
                     partner = wide_ref[n]
-                    back = jnp.zeros((16, LANES), jnp.float32) if first == 0 else pull_ref[n]
+                    if fresh[h]:
+                        back = zero
+                    elif index == 0:
+                        back = before[h][k, at, :]
+                    else:
+                        back = pull_ref[n]
                     for i_m in range(GROUP):
                         term = entry(own[i_m], n) * (held[i_m] - partner)
                         pulls[i_m] += term
                         back -= term
-                    pull_ref[n] = back
-            for i_m in range(GROUP):
-                toward = (held[i_m] - target) * entry(own[i_m], count)
-                there = pl.ds(pl.multiple_of(own[i_m] % local * rows + i * 16, 16), 16)
-                out_ref[slot[own[i_m] // local], there, :] = weight * (toward - pulls[i_m] * share)
+                    if h in after and index == len(turn) - 1:
+                        after[h][k, at, :] = back
+                    else:
+                        pull_ref[n] = back
+                fresh[h] = False
+            for k in range(GROUP):
+                toward = (held[k] - target) * entry(own[k], count)
+                there = pl.ds(pl.multiple_of(k * rows + i * 16, 16), 16)
+                out_refs[g][there, :] = weight * (toward - pulls[k] * share)
         return carry
 
     lax.fori_loop(0, rows // 16, slab, 0)
 
 
-def restore_kernel(degrees, lines, x_ref, out_ref, held_ref, sems):
+def restore_kernel(degrees, lines, shifts, *refs):
+    *x_refs, out_ref, held_ref, sems = refs
     local, each, _ = held_ref.shape
-    channels = x_ref.shape[0]
+    channels = len(x_refs)
     rows = each // channels
     run = rows // lines
+    me = lax.axis_index("member")
     copies = []
     for m in range(local):
-        for c in range(channels):
-            factor = jnp.exp2(-x_ref[c, local * rows : local * rows + 1, :]) * (2.0 * degrees)
+        for x_ref, shift in zip(x_refs, shifts):
+            factor = jnp.exp2(-x_ref[local * rows : local * rows + 1, :]) * (2.0 * degrees)
             for line in range(lines):
                 at = m * rows + line * run
-                to = (line * channels + c) * run
-                held_ref[m, to : to + run, :] = x_ref[c, at : at + run, :] * factor
+                to = pl.multiple_of(line * channels * run + jnp.bitwise_xor(me, shift) * run, 4)
+                held_ref[m, pl.ds(to, run), :] = x_ref[at : at + run, :] * factor
         copy = pltpu.make_async_copy(held_ref.at[m], out_ref.at[pl.ds(m * each, each)], sems.at[m])
         copy.start()
         copies.append(copy)
@@ -252,7 +280,8 @@
     rows = lines * parts * tiles
     degrees = degree_weight.shape[0]
     shifts = (0, 4, 6, 2, 5, 7, 1, 3)
-    stages = [[0, 1, 2], [3], [4], [5, 6], [7]]
+    turns = [[1, 2, 4], [6, 7, 3, 5, 0]]
+    stages = [[0, 1, 2], [3], [4, 5], [6, 7]]
     plans, place, entries = pair_table(stages, local, count)
     vmem = pltpu.CompilerParams(vmem_limit_bytes=16 << 20)
     whole = pl.BlockSpec(memory_space=pltpu.VMEM)
@@ -304,25 +333,37 @@
         scaled = scaled + list(result[1 : 1 + len(fresh)])
         if first:
             against = result[-1]
-    got = lax.all_to_all(jnp.broadcast_to(sums[-1][None], (spread, 8, LANES)), "order", 0, 0, tiled=True)
-
-    gradient = pl.pallas_call(
-        functools.partial(gradient_kernel, place, count, shifts),
-        out_shape=jax.ShapeDtypeStruct((groups, local * rows + 16, LANES), jnp.float32),
-        scratch_shapes=[
-            pltpu.VMEM((entries, LANES), jnp.float32),
-            pltpu.VMEM((count, 16, LANES), jnp.float32),
-            pltpu.VMEM((count, 16, LANES), jnp.float32),
-        ],
-        compiler_params=vmem,
-        name="gradients",
-    )(got, *held, target, drawn)
-
-    back = lax.all_to_all(gradient.astype(jnp.float16), "member", 0, 0, tiled=True).astype(jnp.float32)
+    pair = sums[-1] + lax.ppermute(sums[-1], "order", [(i, i ^ 1) for i in range(spread)])
+    alike = [list(range(core, spread, 2)) for core in range(2)]
+    got = jnp.broadcast_to(pair[None], (spread // 2, 8, LANES))
+    got = lax.all_to_all(got, "order", 0, 0, tiled=True, axis_index_groups=alike)
+
+    back, source, pulled = [None] * groups, (got,), {}
+    for turn in turns:
+        first = not pulled
+        rest = [g for g in range(groups) if g not in turn] if first else []
+        result = pl.pallas_call(
+            functools.partial(gradient_kernel, place, count, turn, rest, first),
+            out_shape=(jax.ShapeDtypeStruct((local * rows + 16, LANES), jnp.float32),) * len(turn)
+            + (jax.ShapeDtypeStruct((local, rows, LANES), jnp.float32),) * len(rest)
+            + ((jax.ShapeDtypeStruct((entries, LANES), jnp.float32), jax.ShapeDtypeStruct((16, LANES), jnp.float32)) if first else ()),
+            scratch_shapes=[
+                pltpu.VMEM((count, 16, LANES), jnp.float32),
+                pltpu.VMEM((count, 16, LANES), jnp.float32),
+            ],
+            compiler_params=vmem,
+            name="gradients",
+        )(*source, *held, target, drawn, *(pulled[g] for g in turn if not first))
+        if first:
+            pulled = dict(zip(rest, result[len(turn) :]))
+            source = result[-2:]
+        for g, block in zip(turn, result):
+            if shifts[g]:
+                block = lax.ppermute(block.astype(jnp.float16), "member", [(i, i ^ shifts[g]) for i in range(groups)])
+            back[g] = block.astype(jnp.float32)
     back = pl.pallas_call(
-        functools.partial(restore_kernel, degrees, lines),
+        functools.partial(restore_kernel, degrees, lines, shifts),
         out_shape=jax.ShapeDtypeStruct((local * rows * channels, LANES), jnp.float32),
-        in_specs=[whole],
         out_specs=outside,
         scratch_shapes=[
             pltpu.VMEM((local, rows * channels, LANES), jnp.float32),
@@ -330,7 +371,7 @@
         ],
         compiler_params=vmem,
         name="restore",
-    )(back)
+    )(*back)
     return from_rows(back.reshape(local * lines * channels, tiles, parts, LANES)).reshape(members.shape)
 
 

time: 73.4 us -> 70.5 us (0.960)
  blocking collectives: 42.2 us -> 19.8 us
  starting transfers between devices: 11.1 us -> 22.4 us
  waiting for transfers between devices: 4.58 us -> 12.6 us
    all_to_all x2 -> x1, blocking collectives: 42.2 us -> 19.8 us  [on_device(): lax.all_to_all(got, 'order', 0, 0, tiled=True, axis_index_groups=alike)]
    ppermute x0 -> x8, starting transfers between devices: none -> 11.7 us  [the longest x7 11.7 us: on_device(): lax.ppermute(block.astype(jnp.float16), 'member', [(i, i ^ shifts[g]) for...]
    ppermute x0 -> x8, waiting for transfers between devices: none -> 7.86 us  [the longest x7 6.7 us: on_device(): lax.ppermute(block.astype(jnp.float16), 'member', [(i, i ^ shifts[g]) for...]
    pallas_call x2 -> x3, Pallas kernels: 7.35 us -> 7.8 us  [the longest x2 6.3 us: on_device(): pl.pallas_call(functools.partial(gradient_kernel, place, count, turn, res...]
    pallas_call x5 -> x4, Pallas kernels: 5.23 us -> 5.09 us  [on_device(): pl.pallas_call(functools.partial(distance_kernel, plan, len(scaled), len(...]
  transfers between devices with their start and end apart: 7 -> 15, of which waited for: 3 -> 8; matrix products, arithmetic and copies ran while one was open for 0% -> 0% of each run, Pallas kernels for 5% -> 8%
where the time goes in v3:
time: 70.5 us; the launch traced here: 70.4 us
  starting transfers between devices  22.4 us (32%)
  blocking collectives  19.8 us (28%)
  Pallas kernels  14.9 us (21%)
  waiting for transfers between devices  12.6 us (18%)
    all_to_all x1, blocking collectives, on_device(): lax.all_to_all(got, 'order', 0, 0, tiled=True, axis_index_groups=alike)  19.8 us
    ppermute x7, starting transfers between devices, on_device(): lax.ppermute(block.astype(jnp.float16), 'member', [(i, i ^ shifts[g]) for...  11.7 us
    ppermute x7, starting transfers between devices, on_device(): lax.ppermute(block, 'member', [(i, i ^ shifts[step]) for i in range(group...  10.7 us
    ppermute x7, waiting for transfers between devices, on_device(): lax.ppermute(block.astype(jnp.float16), 'member', [(i, i ^ shifts[g]) for...  6.7 us
    pallas_call x2, Pallas kernels, on_device(): pl.pallas_call(functools.partial(gradient_kernel, place, count, turn, res...  6.3 us
    pallas_call x4, Pallas kernels, on_device(): pl.pallas_call(functools.partial(distance_kernel, plan, len(scaled), len(...  5.09 us
    ppermute x7, waiting for transfers between devices, on_device(): lax.ppermute(block, 'member', [(i, i ^ shifts[step]) for i in range(group...  4.79 us
    pallas_call x1, Pallas kernels, on_device(): pl.pallas_call(functools.partial(prepare_kernel, degrees, shifts), out_sh...  1.97 us
  transfers between devices with their start and end apart: 15, of which 8 were waited for; matrix products, arithmetic and copies ran while one was open for 0% of the time, Pallas kernels for 8%

profile of v3, /device:TPU:8, one launch (start us, length us, event | category | flops | bytes accessed | tf_op | source)
XLA Modules:
  0.0 70.4 jit_solution(12478422427244135250)
XLA Ops:
  0.0 2.0 %prepare.1 = (bf16[4,12,2,768]{3,2,1,0:T(2,128)(2,1)S(1)}, bf16[4,12,2,768]{3,2,1,0:T(2,128)(2,1)S(1)}, bf16[4,12,2,768]{3,2,1,0:T(2,128)(2,1)S(1)}, bf16[4,12,2...) custom-call(bf16[4,12,8,2,768]{4,3,2,1,0:T(2,128)(2,1)} %x_ref.1, ...), custom_call_target="tpu_custom_call" | custom-call | tf_op jit(solution)/shard_map/prepare/pallas_call | solution.py:291
  2.0 2.3 %collective-permute-start = (bf16[4,12,2,768]{3,2,1,0:T(2,128)(2,1)S(1)}, bf16[4,12,2,768]{3,2,1,0:T(2,128)(2,1)S(1)}, u32[]{:S(2)}, u32[]{:S(2)}) collective-permute-start(bf16[4,12,2,768]{3,2,1,0:T(2,128)(2,1)S(1)} %get-tuple-element.49), channel_id=1, source_target_pairs={{0,4},{1,5},{2,6},{3,7},{4,0},{5,1},{6,2},{7,3},{8,12},{9,13},{10,... | collective-permute-start | bytes 442376 | tf_op jit(solution)/shard_map/ppermute | solution.py:315
  4.2 2.3 %collective-permute-start.1 = (bf16[4,12,2,768]{3,2,1,0:T(2,128)(2,1)S(1)}, bf16[4,12,2,768]{3,2,1,0:T(2,128)(2,1)S(1)}, u32[]{:S(2)}, u32[]{:S(2)}) collective-permute-start(bf16[4,12,2,768]{3,2,1,0:T(2,128)(2,1)S(1)} %get-tuple-element.52), channel_id=1, source_target_pairs={{0,6},{1,7},{2,4},{3,5},{4,2},{5,3},{6,0},{7,1},{8,14},{9,15},{10,... | collective-permute-start | bytes 442376 | tf_op jit(solution)/shard_map/ppermute | solution.py:315
  6.5 0.8 %collective-permute-start.2 = (bf16[4,12,2,768]{3,2,1,0:T(2,128)(2,1)S(1)}, bf16[4,12,2,768]{3,2,1,0:T(2,128)(2,1)S(1)}, u32[]{:S(2)}, u32[]{:S(2)}) collective-permute-start(bf16[4,12,2,768]{3,2,1,0:T(2,128)(2,1)S(1)} %get-tuple-element.58), channel_id=1, source_target_pairs={{0,2},{1,3},{2,0},{3,1},{4,6},{5,7},{6,4},{7,5},{8,10},{9,11},{10,... | collective-permute-start | bytes 442376 | tf_op jit(solution)/shard_map/ppermute | solution.py:315
  7.3 1.1 %collective-permute-start.3 = (bf16[4,12,2,768]{3,2,1,0:T(2,128)(2,1)S(1)}, bf16[4,12,2,768]{3,2,1,0:T(2,128)(2,1)S(1)}, u32[]{:S(2)}, u32[]{:S(2)}) collective-permute-start(bf16[4,12,2,768]{3,2,1,0:T(2,128)(2,1)S(1)} %get-tuple-element.61), channel_id=1, source_target_pairs={{0,5},{1,4},{2,7},{3,6},{4,1},{5,0},{6,3},{7,2},{8,13},{9,12},{10,... | collective-permute-start | bytes 442376 | tf_op jit(solution)/shard_map/ppermute | solution.py:315
  8.4 3.1 %collective-permute-start.4 = (bf16[4,12,2,768]{3,2,1,0:T(2,128)(2,1)S(1)}, bf16[4,12,2,768]{3,2,1,0:T(2,128)(2,1)S(1)}, u32[]{:S(2)}, u32[]{:S(2)}) collective-permute-start(bf16[4,12,2,768]{3,2,1,0:T(2,128)(2,1)S(1)} %get-tuple-element.62), channel_id=1, source_target_pairs={{0,7},{1,6},{2,5},{3,4},{4,3},{5,2},{6,1},{7,0},{8,15},{9,14},{10,... | collective-permute-start | bytes 442376 | tf_op jit(solution)/shard_map/ppermute | solution.py:315
  11.5 0.0 collective-permute-done
  11.5 1.1 %collective-permute-start.6 = (bf16[4,12,2,768]{3,2,1,0:T(2,128)(2,1)S(1)}, bf16[4,12,2,768]{3,2,1,0:T(2,128)(2,1)S(1)}, u32[]{:S(2)}, u32[]{:S(2)}) collective-permute-start(bf16[4,12,2,768]{3,2,1,0:T(2,128)(2,1)S(1)} %get-tuple-element.66), channel_id=1, source_target_pairs={{0,3},{1,2},{2,1},{3,0},{4,7},{5,6},{6,5},{7,4},{8,11},{9,10},{10,... | collective-permute-start | bytes 442376 | tf_op jit(solution)/shard_map/ppermute | solution.py:315
  12.7 0.9 %collective-permute-done.1 = bf16[4,12,2,768]{3,2,1,0:T(2,128)(2,1)S(1)} collective-permute-done((bf16[4,12,2,768]{3,2,1,0:T(2,128)(2,1)S(1)}, bf16[4,12,2,768]{3,2,1,0:T(2,128)(2,1)S(1)}, u32[]{:S(2)}, u32[]{:S(2)}) %collective-permute-start.1) | collective-permute-done | bytes 147488 | tf_op jit(solution)/shard_map/ppermute | solution.py:315
  13.6 0.0 collective-permute-start.5
  13.6 0.8 %distances.4 = (f32[1,128]{1,0:T(1,128)S(1)}, f32[4,144,128]{2,1,0:T(8,128)S(1)}, f32[4,144,128]{2,1,0:T(8,128)S(1)}, f32[4,144,128]{2,1,0:T(8,128)S(1)}, f32[144,128]{1,0:T(8,128)S(1)}) custom-call(bf16[4,144,128]{2,1,0:T(8,128)(2,1)S(1)} %bitcast.65, bf16[4,144,128]{2,1,0:T(8,128)(2,1)S(1)} %bitcast.68, bf16[4,144,128]{2,1,0:T(8,128)(2,1)S(1)} %bitcast.71, ...), custom_call_target="tpu_custom_call" | custom-call | tf_op jit(solution)/shard_map/distances/pallas_call | solution.py:325
  14.4 0.4 collective-permute-done.2
  14.8 0.7 distances.5
  15.5 3.3 %collective-permute-done.3 = bf16[4,12,2,768]{3,2,1,0:T(2,128)(2,1)S(1)} collective-permute-done((bf16[4,12,2,768]{3,2,1,0:T(2,128)(2,1)S(1)}, bf16[4,12,2,768]{3,2,1,0:T(2,128)(2,1)S(1)}, u32[]{:S(2)}, u32[]{:S(2)}) %collective-permute-start.3) | collective-permute-done | bytes 147488 | tf_op jit(solution)/shard_map/ppermute | solution.py:315
  18.8 0.2 collective-permute-done.4
  19.0 1.5 %distances.6 = (f32[2,128]{1,0:T(2,128)S(1)}, f32[4,144,128]{2,1,0:T(8,128)S(1)}, f32[4,144,128]{2,1,0:T(8,128)S(1)}) custom-call(f32[4,144,128]{2,1,0:T(8,128)S(1)} %get-tuple-element.55.refs_0_, f32[4,144,128]{2,1,0:T(8,128)S(1)} %get-tuple-element.56.refs_1_, f32[4,144,128]{2,1,0:T(8,128)S(1)} %get-tuple-element.57.refs_2_, ...), custom_call_target="tpu_custom_call" | custom-call | tf_op jit(solution)/shard_map/distances/pallas_call | solution.py:325
  20.4 0.0 collective-permute-done.6
  20.4 0.0 collective-permute-done.5
  20.4 2.1 %distances.7 = (f32[8,128]{1,0:T(8,128)S(1)}, f32[4,144,128]{2,1,0:T(8,128)}, f32[4,144,128]{2,1,0:T(8,128)}) custom-call(f32[4,144,128]{2,1,0:T(8,128)S(1)} %get-tuple-element.55.refs_0_, f32[4,144,128]{2,1,0:T(8,128)S(1)} %get-tuple-element.56.refs_1_, f32[4,144,128]{2,1,0:T(8,128)S(1)} %get-tuple-element.57.refs_2_, ...), custom_call_target="tpu_custom_call" | custom-call | tf_op jit(solution)/shard_map/distances/pallas_call | solution.py:325
  22.6 0.0 collective-permute-start.7
  22.6 1.2 %collective-permute-done.7 = f32[8,128]{1,0:T(8,128)S(1)} collective-permute-done((f32[8,128]{1,0:T(8,128)S(1)}, f32[8,128]{1,0:T(8,128)S(1)}, u32[]{:S(2)}, u32[]{:S(2)}) %collective-permute-start.7) | collective-permute-done | bytes 4128 | tf_op jit(solution)/shard_map/ppermute | solution.py:336
  23.8 19.8 %all_to_all.5.refs_0_ = f32[16,8,128]{2,1,0:T(8,128)S(1)} all-to-all(f32[16,8,128]{2,1,0:T(8,128)S(1)} %broadcast_in_dim.2), channel_id=1, replica_groups={{0,16,32,48,64,80,96,112,128,144,160,176,192,208,224,240},{8,24,40,56,7..., dimensions={0} | all-to-all | bytes 131072 | tf_op jit(solution)/shard_map/all_to_all | solution.py:339
  43.6 3.9 %gradients.2 = (f32[592,128]{1,0:T(8,128)S(1)}, f32[592,128]{1,0:T(8,128)S(1)}, f32[592,128]{1,0:T(8,128)S(1)}, f32[4,144,128]{2,1,0:T(8,128)S(1)}, f32[4,144,12...) custom-call(f32[16,8,128]{2,1,0:T(8,128)S(1)} %all_to_all.5.refs_0_,, ...), custom_call_target="tpu_custom_call" | custom-call | tf_op jit(solution)/shard_map/gradients/pallas_call | solution.py:345
  47.5 2.8 %collective-permute-start.11 = (f16[592,128]{1,0:T(8,128)(2,1)S(1)}, f16[592,128]{1,0:T(8,128)(2,1)S(1)}, u32[]{:S(2)}, u32[]{:S(2)}) collective-permute-start(f16[592,128]{1,0:T(8,128)(2,1)S(1)} %convert_element_type.48), channel_id=1, source_target_pairs={{0,5},{1,4},{2,7},{3,6},{4,1},{5,0},{6,3},{7,2},{8,13},{9,12},{10,... | collective-permute-start | bytes 454664 | tf_op jit(solution)/shard_map/ppermute | solution.py:362
  50.4 2.1 %collective-permute-start.9 = (f16[592,128]{1,0:T(8,128)(2,1)S(1)}, f16[592,128]{1,0:T(8,128)(2,1)S(1)}, u32[]{:S(2)}, u32[]{:S(2)}) collective-permute-start(f16[592,128]{1,0:T(8,128)(2,1)S(1)} %convert_element_type.44), channel_id=1, source_target_pairs={{0,6},{1,7},{2,4},{3,5},{4,2},{5,3},{6,0},{7,1},{8,14},{9,15},{10,... | collective-permute-start | bytes 454664 | tf_op jit(solution)/shard_map/ppermute | solution.py:362
  52.5 2.4 %gradients.3 = (f32[592,128]{1,0:T(8,128)S(1)}, f32[592,128]{1,0:T(8,128)S(1)}, f32[592,128]{1,0:T(8,128)S(1)}, f32[592,128]{1,0:T(8,128)S(1)}, f32[592,128]{1,0:T(8,128)S(1)}) custom-call(f32[768,128]{1,0:T(8,128)S(1)} %get-tuple-element.72.refs_0_, f32[16,128]{1,0:T(8,128)S(1)} %get-tuple-element.73.refs_1_, bf16[4,144,128]{2,1,0:T(8,128)(2,1)S(1)} %bitcast.67, ...), custom_call_target="tpu_custom_call" | custom-call | tf_op jit(solution)/shard_map/gradients/pallas_call | solution.py:345
  55.1 1.6 %collective-permute-start.8 = (f16[592,128]{1,0:T(8,128)(2,1)S(1)}, f16[592,128]{1,0:T(8,128)(2,1)S(1)}, u32[]{:S(2)}, u32[]{:S(2)}) collective-permute-start(f16[592,128]{1,0:T(8,128)(2,1)S(1)} %convert_element_type.42), channel_id=1, source_target_pairs={{0,4},{1,5},{2,6},{3,7},{4,0},{5,1},{6,2},{7,3},{8,12},{9,13},{10,... | collective-permute-start | bytes 454664 | tf_op jit(solution)/shard_map/ppermute | solution.py:362
  56.7 1.3 %collective-permute-start.14 = (f16[592,128]{1,0:T(8,128)(2,1)S(1)}, f16[592,128]{1,0:T(8,128)(2,1)S(1)}, u32[]{:S(2)}, u32[]{:S(2)}) collective-permute-start(f16[592,128]{1,0:T(8,128)(2,1)S(1)} %convert_element_type.54), channel_id=1, source_target_pairs={{0,3},{1,2},{2,1},{3,0},{4,7},{5,6},{6,5},{7,4},{8,11},{9,10},{10,... | collective-permute-start | bytes 454664 | tf_op jit(solution)/shard_map/ppermute | solution.py:362
  58.0 0.3 collective-permute-start.13
  58.4 0.0 collective-permute-done.11
  58.4 1.9 %collective-permute-start.12 = (f16[592,128]{1,0:T(8,128)(2,1)S(1)}, f16[592,128]{1,0:T(8,128)(2,1)S(1)}, u32[]{:S(2)}, u32[]{:S(2)}) collective-permute-start(f16[592,128]{1,0:T(8,128)(2,1)S(1)} %convert_element_type.50), channel_id=1, source_target_pairs={{0,7},{1,6},{2,5},{3,4},{4,3},{5,2},{6,1},{7,0},{8,15},{9,14},{10,... | collective-permute-start | bytes 454664 | tf_op jit(solution)/shard_map/ppermute | solution.py:362
  60.3 0.0 collective-permute-done.9
  60.3 1.6 %collective-permute-start.10 = (f16[592,128]{1,0:T(8,128)(2,1)S(1)}, f16[592,128]{1,0:T(8,128)(2,1)S(1)}, u32[]{:S(2)}, u32[]{:S(2)}) collective-permute-start(f16[592,128]{1,0:T(8,128)(2,1)S(1)} %convert_element_type.46), channel_id=1, source_target_pairs={{0,2},{1,3},{2,0},{3,1},{4,6},{5,7},{6,4},{7,5},{8,10},{9,11},{10,... | collective-permute-start | bytes 454664 | tf_op jit(solution)/shard_map/ppermute | solution.py:362
  61.9 1.1 %collective-permute-done.8 = f16[592,128]{1,0:T(8,128)(2,1)S(1)} collective-permute-done((f16[592,128]{1,0:T(8,128)(2,1)S(1)}, f16[592,128]{1,0:T(8,128)(2,1)S(1)}, u32[]{:S(2)}, u32[]{:S(2)}) %collective-permute-start.8) | collective-permute-done | bytes 151584 | tf_op jit(solution)/shard_map/ppermute | solution.py:362
  63.0 1.8 %collective-permute-done.14 = f16[592,128]{1,0:T(8,128)(2,1)S(1)} collective-permute-done((f16[592,128]{1,0:T(8,128)(2,1)S(1)}, f16[592,128]{1,0:T(8,128)(2,1)S(1)}, u32[]{:S(2)}, u32[]{:S(2)}) %collective-permute-start.14) | collective-permute-done | bytes 151584 | tf_op jit(solution)/shard_map/ppermute | solution.py:362
  64.9 0.0 collective-permute-done.13
  64.9 3.7 %collective-permute-done.12 = f16[592,128]{1,0:T(8,128)(2,1)S(1)} collective-permute-done((f16[592,128]{1,0:T(8,128)(2,1)S(1)}, f16[592,128]{1,0:T(8,128)(2,1)S(1)}, u32[]{:S(2)}, u32[]{:S(2)}) %collective-permute-start.12) | collective-permute-done | bytes 151584 | tf_op jit(solution)/shard_map/ppermute | solution.py:362
  68.7 0.0 collective-permute-done.10
  68.7 1.5 %restore.1 = f32[4608,128]{1,0:T(8,128)} custom-call(f32[592,128]{1,0:T(8,128)S(1)} %get-tuple-element.79.refs_0_, f32[592,128]{1,0:T(8,128)S(1)} %convert_element_type.43.refs_1_, f32[592,128]{1,0:T(8,128)S(1)} %convert_element_type.45.refs_2_, f32[592,128]{1,0:T(8,128)S(1)} %convert_element_type.47.refs_3_, f32[592,128]{1,0:T(8,128)S(1)} %convert_element_type.49.refs_4_, ...), custom_call_target="tpu_custom_call" | custom-call | tf_op jit(solution)/shard_map/restore/pallas_call | solution.py:364
  (16 shorter events, 0.3 us)
Async XLA Ops:
  2.0 9.6 %collective-permute-start = (bf16[4,12,2,768]{3,2,1,0:T(2,128)(2,1)S(1)}, bf16[4,12,2,768]{3,2,1,0:T(2,128)(2,1)S(1)}, u32[]{:S(2)}, u32[]{:S(2)}) collective-permute-start(bf16[4,12,2,768]{3,2,1,0:T(2,128)(2,1)S(1)} %get-tuple-element.49), channel_id=1, source_target_pairs={{0,4},{1,5},{2,6},{3,7},{4,0},{5,1},{6,2},{7,3},{8,12},{9,13},{10,... | collective-permute-start | bytes 442376 | tf_op jit(solution)/shard_map/ppermute | solution.py:315
  4.2 9.4 %collective-permute-start.1 = (bf16[4,12,2,768]{3,2,1,0:T(2,128)(2,1)S(1)}, bf16[4,12,2,768]{3,2,1,0:T(2,128)(2,1)S(1)}, u32[]{:S(2)}, u32[]{:S(2)}) collective-permute-start(bf16[4,12,2,768]{3,2,1,0:T(2,128)(2,1)S(1)} %get-tuple-element.52), channel_id=1, source_target_pairs={{0,6},{1,7},{2,4},{3,5},{4,2},{5,3},{6,0},{7,1},{8,14},{9,15},{10,... | collective-permute-start | bytes 442376 | tf_op jit(solution)/shard_map/ppermute | solution.py:315
  6.5 8.3 %collective-permute-start.2 = (bf16[4,12,2,768]{3,2,1,0:T(2,128)(2,1)S(1)}, bf16[4,12,2,768]{3,2,1,0:T(2,128)(2,1)S(1)}, u32[]{:S(2)}, u32[]{:S(2)}) collective-permute-start(bf16[4,12,2,768]{3,2,1,0:T(2,128)(2,1)S(1)} %get-tuple-element.58), channel_id=1, source_target_pairs={{0,2},{1,3},{2,0},{3,1},{4,6},{5,7},{6,4},{7,5},{8,10},{9,11},{10,... | collective-permute-start | bytes 442376 | tf_op jit(solution)/shard_map/ppermute | solution.py:315
  7.3 11.4 %collective-permute-start.3 = (bf16[4,12,2,768]{3,2,1,0:T(2,128)(2,1)S(1)}, bf16[4,12,2,768]{3,2,1,0:T(2,128)(2,1)S(1)}, u32[]{:S(2)}, u32[]{:S(2)}) collective-permute-start(bf16[4,12,2,768]{3,2,1,0:T(2,128)(2,1)S(1)} %get-tuple-element.61), channel_id=1, source_target_pairs={{0,5},{1,4},{2,7},{3,6},{4,1},{5,0},{6,3},{7,2},{8,13},{9,12},{10,... | collective-permute-start | bytes 442376 | tf_op jit(solution)/shard_map/ppermute | solution.py:315
  8.4 10.5 %collective-permute-start.4 = (bf16[4,12,2,768]{3,2,1,0:T(2,128)(2,1)S(1)}, bf16[4,12,2,768]{3,2,1,0:T(2,128)(2,1)S(1)}, u32[]{:S(2)}, u32[]{:S(2)}) collective-permute-start(bf16[4,12,2,768]{3,2,1,0:T(2,128)(2,1)S(1)} %get-tuple-element.62), channel_id=1, source_target_pairs={{0,7},{1,6},{2,5},{3,4},{4,3},{5,2},{6,1},{7,0},{8,15},{9,14},{10,... | collective-permute-start | bytes 442376 | tf_op jit(solution)/shard_map/ppermute | solution.py:315
  11.5 8.9 %collective-permute-start.6 = (bf16[4,12,2,768]{3,2,1,0:T(2,128)(2,1)S(1)}, bf16[4,12,2,768]{3,2,1,0:T(2,128)(2,1)S(1)}, u32[]{:S(2)}, u32[]{:S(2)}) collective-permute-start(bf16[4,12,2,768]{3,2,1,0:T(2,128)(2,1)S(1)} %get-tuple-element.66), channel_id=1, source_target_pairs={{0,3},{1,2},{2,1},{3,0},{4,7},{5,6},{6,5},{7,4},{8,11},{9,10},{10,... | collective-permute-start | bytes 442376 | tf_op jit(solution)/shard_map/ppermute | solution.py:315
  13.6 6.8 %collective-permute-start.5 = (bf16[4,12,2,768]{3,2,1,0:T(2,128)(2,1)S(1)}, bf16[4,12,2,768]{3,2,1,0:T(2,128)(2,1)S(1)}, u32[]{:S(2)}, u32[]{:S(2)}) collective-permute-start(bf16[4,12,2,768]{3,2,1,0:T(2,128)(2,1)S(1)} %get-tuple-element.65), channel_id=1, source_target_pairs={{0,1},{1,0},{2,3},{3,2},{4,5},{5,4},{6,7},{7,6},{8,9},{9,8},{10,11... | collective-permute-start | bytes 442376 | tf_op jit(solution)/shard_map/ppermute | solution.py:315
  22.6 1.2 %collective-permute-start.7 = (f32[8,128]{1,0:T(8,128)S(1)}, f32[8,128]{1,0:T(8,128)S(1)}, u32[]{:S(2)}, u32[]{:S(2)}) collective-permute-start(f32[8,128]{1,0:T(8,128)S(1)} %get-tuple-element.70), channel_id=1, source_target_pairs={{0,8},{8,0},{16,24},{24,16},{32,40},{40,32},{48,56},{56,48},{64,72... | collective-permute-start | bytes 12296 | tf_op jit(solution)/shard_map/ppermute | solution.py:336
  47.5 10.9 %collective-permute-start.11 = (f16[592,128]{1,0:T(8,128)(2,1)S(1)}, f16[592,128]{1,0:T(8,128)(2,1)S(1)}, u32[]{:S(2)}, u32[]{:S(2)}) collective-permute-start(f16[592,128]{1,0:T(8,128)(2,1)S(1)} %convert_element_type.48), channel_id=1, source_target_pairs={{0,5},{1,4},{2,7},{3,6},{4,1},{5,0},{6,3},{7,2},{8,13},{9,12},{10,... | collective-permute-start | bytes 454664 | tf_op jit(solution)/shard_map/ppermute | solution.py:362
  50.4 9.9 %collective-permute-start.9 = (f16[592,128]{1,0:T(8,128)(2,1)S(1)}, f16[592,128]{1,0:T(8,128)(2,1)S(1)}, u32[]{:S(2)}, u32[]{:S(2)}) collective-permute-start(f16[592,128]{1,0:T(8,128)(2,1)S(1)} %convert_element_type.44), channel_id=1, source_target_pairs={{0,6},{1,7},{2,4},{3,5},{4,2},{5,3},{6,0},{7,1},{8,14},{9,15},{10,... | collective-permute-start | bytes 454664 | tf_op jit(solution)/shard_map/ppermute | solution.py:362
  55.1 8.0 %collective-permute-start.8 = (f16[592,128]{1,0:T(8,128)(2,1)S(1)}, f16[592,128]{1,0:T(8,128)(2,1)S(1)}, u32[]{:S(2)}, u32[]{:S(2)}) collective-permute-start(f16[592,128]{1,0:T(8,128)(2,1)S(1)} %convert_element_type.42), channel_id=1, source_target_pairs={{0,4},{1,5},{2,6},{3,7},{4,0},{5,1},{6,2},{7,3},{8,12},{9,13},{10,... | collective-permute-start | bytes 454664 | tf_op jit(solution)/shard_map/ppermute | solution.py:362
  56.7 8.2 %collective-permute-start.14 = (f16[592,128]{1,0:T(8,128)(2,1)S(1)}, f16[592,128]{1,0:T(8,128)(2,1)S(1)}, u32[]{:S(2)}, u32[]{:S(2)}) collective-permute-start(f16[592,128]{1,0:T(8,128)(2,1)S(1)} %convert_element_type.54), channel_id=1, source_target_pairs={{0,3},{1,2},{2,1},{3,0},{4,7},{5,6},{6,5},{7,4},{8,11},{9,10},{10,... | collective-permute-start | bytes 454664 | tf_op jit(solution)/shard_map/ppermute | solution.py:362
  58.0 6.9 %collective-permute-start.13 = (f16[592,128]{1,0:T(8,128)(2,1)S(1)}, f16[592,128]{1,0:T(8,128)(2,1)S(1)}, u32[]{:S(2)}, u32[]{:S(2)}) collective-permute-start(f16[592,128]{1,0:T(8,128)(2,1)S(1)} %convert_element_type.52), channel_id=1, source_target_pairs={{0,1},{1,0},{2,3},{3,2},{4,5},{5,4},{6,7},{7,6},{8,9},{9,8},{10,11... | collective-permute-start | bytes 454664 | tf_op jit(solution)/shard_map/ppermute | solution.py:362
  58.4 10.3 %collective-permute-start.12 = (f16[592,128]{1,0:T(8,128)(2,1)S(1)}, f16[592,128]{1,0:T(8,128)(2,1)S(1)}, u32[]{:S(2)}, u32[]{:S(2)}) collective-permute-start(f16[592,128]{1,0:T(8,128)(2,1)S(1)} %convert_element_type.50), channel_id=1, source_target_pairs={{0,7},{1,6},{2,5},{3,4},{4,3},{5,2},{6,1},{7,0},{8,15},{9,14},{10,... | collective-permute-start | bytes 454664 | tf_op jit(solution)/shard_map/ppermute | solution.py:362
  60.3 8.4 %collective-permute-start.10 = (f16[592,128]{1,0:T(8,128)(2,1)S(1)}, f16[592,128]{1,0:T(8,128)(2,1)S(1)}, u32[]{:S(2)}, u32[]{:S(2)}) collective-permute-start(f16[592,128]{1,0:T(8,128)(2,1)S(1)} %convert_element_type.46), channel_id=1, source_target_pairs={{0,2},{1,3},{2,0},{3,1},{4,6},{5,7},{6,4},{7,5},{8,10},{9,11},{10,... | collective-permute-start | bytes 454664 | tf_op jit(solution)/shard_map/ppermute | solution.py:362

commit v4 on v3

--- a/solution.py
+++ b/solution.py
@@ -104,7 +104,7 @@
             at = (row * parts + part) * 2
             piece = line[0:2, part * LANES : (part + 1) * LANES]
             weight_ref[at : at + 2, :] = piece
-            drawn_ref[at : at + 2, :] = piece * half
+            drawn_ref[at : at + 2, :] = jnp.sqrt(piece) * half
     for copy in out:
         copy.wait()
 
@@ -173,7 +173,7 @@
     out_refs = {g: refs.pop(0) for g in turn}
     after = {g: refs.pop(0) for g in rest}
     if first:
-        table_ref, power_ref, wide_ref, pull_ref = refs
+        table_ref, power_ref, pull_ref = refs
         squares = jnp.sum(from_refs[0][...], axis=0)
         inverse = lax.rsqrt(squares + epsilon)
         largest = jnp.max(squares * inverse * inverse, axis=(0, 1), keepdims=True)
@@ -185,7 +185,7 @@
             column = jnp.broadcast_to(columns[:, block : block + 1], (LANES, LANES))
             table_ref[block * LANES : (block + 1) * LANES, :] = column
     else:
-        wide_ref, pull_ref = refs
+        (pull_ref,) = refs
         table_ref = from_refs[0]
         power = from_refs[1][...]
     rows = w_ref.shape[0]
@@ -197,19 +197,16 @@
         at = place[(min(m, n), max(m, n))]
         return jnp.broadcast_to(table_ref[at : at + 1, :], (16, LANES))
 
-    def slab(i, carry):
-        at = pl.ds(pl.multiple_of(i * 16, 16), 16)
-        for g in turn + rest:
-            for k in range(GROUP):
-                wide_ref[g * GROUP + k] = x_refs[g][k, at, :].astype(jnp.float32)
-        target = y_ref[at, :].astype(jnp.float32)
+    def slab(i):
+        at = slice(i * 16, (i + 1) * 16)
+        target = y_ref[at, :]
         weight = w_ref[at, :] * scale
         share = 1.0 / (count - 1)
         zero = jnp.zeros((16, LANES), jnp.float32)
         fresh = {g: not before for g in turn + rest}
         for index, g in enumerate(turn):
             own = list(range(g * GROUP, (g + 1) * GROUP))
-            held = [wide_ref[m] for m in own]
+            held = [x_refs[g][k, at, :] for k in range(GROUP)]
             if fresh[g]:
                 pulls = [zero] * GROUP
             elif index == 0:
@@ -224,7 +221,7 @@
             for h in turn[index + 1 :] + rest:
                 for k in range(GROUP):
                     n = h * GROUP + k
-                    partner = wide_ref[n]
+                    partner = x_refs[h][k, at, :]
                     if fresh[h]:
                         back = zero
                     elif index == 0:
@@ -242,11 +239,11 @@
                 fresh[h] = False
             for k in range(GROUP):
                 toward = (held[k] - target) * entry(own[k], count)
-                there = pl.ds(pl.multiple_of(k * rows + i * 16, 16), 16)
+                there = slice(k * rows + i * 16, k * rows + (i + 1) * 16)
                 out_refs[g][there, :] = weight * (toward - pulls[k] * share)
-        return carry
-
-    lax.fori_loop(0, rows // 16, slab, 0)
+
+    for i in range(rows // 16):
+        slab(i)
 
 
 def restore_kernel(degrees, lines, shifts, *refs):
@@ -347,13 +344,10 @@
             out_shape=(jax.ShapeDtypeStruct((local * rows + 16, LANES), jnp.float32),) * len(turn)
             + (jax.ShapeDtypeStruct((local, rows, LANES), jnp.float32),) * len(rest)
             + ((jax.ShapeDtypeStruct((entries, LANES), jnp.float32), jax.ShapeDtypeStruct((16, LANES), jnp.float32)) if first else ()),
-            scratch_shapes=[
-                pltpu.VMEM((count, 16, LANES), jnp.float32),
-                pltpu.VMEM((count, 16, LANES), jnp.float32),
-            ],
+            scratch_shapes=[pltpu.VMEM((count, 16, LANES), jnp.float32)],
             compiler_params=vmem,
             name="gradients",
-        )(*source, *held, target, drawn, *(pulled[g] for g in turn if not first))
+        )(*source, *scaled, against, drawn, *(pulled[g] for g in turn if not first))
         if first:
             pulled = dict(zip(rest, result[len(turn) :]))
             source = result[-2:]

time: 70.5 us -> 69.9 us (level)
  no operation moved by 1% of the time
where the time goes in v4:
time: 69.9 us; the launch traced here: 69.8 us
  starting transfers between devices  22.3 us (32%)
  blocking collectives  19.8 us (28%)
  Pallas kernels  14.4 us (21%)
  waiting for transfers between devices  12.6 us (18%)
    all_to_all x1, blocking collectives, on_device(): lax.all_to_all(got, 'order', 0, 0, tiled=True, axis_index_groups=alike)  19.8 us
    ppermute x7, starting transfers between devices, on_device(): lax.ppermute(block.astype(jnp.float16), 'member', [(i, i ^ shifts[g]) for...  11.5 us
    ppermute x7, starting transfers between devices, on_device(): lax.ppermute(block, 'member', [(i, i ^ shifts[step]) for i in range(group...  10.7 us
    ppermute x7, waiting for transfers between devices, on_device(): lax.ppermute(block.astype(jnp.float16), 'member', [(i, i ^ shifts[g]) for...  6.7 us
    pallas_call x2, Pallas kernels, on_device(): pl.pallas_call(functools.partial(gradient_kernel, place, count, turn, res...  5.95 us
    pallas_call x4, Pallas kernels, on_device(): pl.pallas_call(functools.partial(distance_kernel, plan, len(scaled), len(...  4.92 us
    ppermute x7, waiting for transfers between devices, on_device(): lax.ppermute(block, 'member', [(i, i ^ shifts[step]) for i in range(group...  4.78 us
    pallas_call x1, Pallas kernels, on_device(): pl.pallas_call(functools.partial(prepare_kernel, degrees, shifts), out_sh...  2.02 us
  transfers between devices with their start and end apart: 15, of which 8 were waited for; matrix products, arithmetic and copies ran while one was open for 0% of the time, Pallas kernels for 8%

profile of v4, /device:TPU:8, one launch (start us, length us, event | category | flops | bytes accessed | tf_op | source)
XLA Modules:
  0.0 69.8 jit_solution(6746211536186961152)
XLA Ops:
  0.0 2.0 %prepare.1 = (bf16[4,12,2,768]{3,2,1,0:T(2,128)(2,1)S(1)}, bf16[4,12,2,768]{3,2,1,0:T(2,128)(2,1)S(1)}, bf16[4,12,2,768]{3,2,1,0:T(2,128)(2,1)S(1)}, bf16[4,12,2...) custom-call(bf16[4,12,8,2,768]{4,3,2,1,0:T(2,128)(2,1)} %x_ref.1, ...), custom_call_target="tpu_custom_call" | custom-call | tf_op jit(solution)/shard_map/prepare/pallas_call | solution.py:288
  2.0 2.3 %collective-permute-start = (bf16[4,12,2,768]{3,2,1,0:T(2,128)(2,1)S(1)}, bf16[4,12,2,768]{3,2,1,0:T(2,128)(2,1)S(1)}, u32[]{:S(2)}, u32[]{:S(2)}) collective-permute-start(bf16[4,12,2,768]{3,2,1,0:T(2,128)(2,1)S(1)} %get-tuple-element.51), channel_id=1, source_target_pairs={{0,4},{1,5},{2,6},{3,7},{4,0},{5,1},{6,2},{7,3},{8,12},{9,13},{10,... | collective-permute-start | bytes 442376 | tf_op jit(solution)/shard_map/ppermute | solution.py:312
  4.3 2.3 %collective-permute-start.1 = (bf16[4,12,2,768]{3,2,1,0:T(2,128)(2,1)S(1)}, bf16[4,12,2,768]{3,2,1,0:T(2,128)(2,1)S(1)}, u32[]{:S(2)}, u32[]{:S(2)}) collective-permute-start(bf16[4,12,2,768]{3,2,1,0:T(2,128)(2,1)S(1)} %get-tuple-element.54), channel_id=1, source_target_pairs={{0,6},{1,7},{2,4},{3,5},{4,2},{5,3},{6,0},{7,1},{8,14},{9,15},{10,... | collective-permute-start | bytes 442376 | tf_op jit(solution)/shard_map/ppermute | solution.py:312
  6.6 0.8 %collective-permute-start.2 = (bf16[4,12,2,768]{3,2,1,0:T(2,128)(2,1)S(1)}, bf16[4,12,2,768]{3,2,1,0:T(2,128)(2,1)S(1)}, u32[]{:S(2)}, u32[]{:S(2)}) collective-permute-start(bf16[4,12,2,768]{3,2,1,0:T(2,128)(2,1)S(1)} %get-tuple-element.60), channel_id=1, source_target_pairs={{0,2},{1,3},{2,0},{3,1},{4,6},{5,7},{6,4},{7,5},{8,10},{9,11},{10,... | collective-permute-start | bytes 442376 | tf_op jit(solution)/shard_map/ppermute | solution.py:312
  7.4 1.1 %collective-permute-start.3 = (bf16[4,12,2,768]{3,2,1,0:T(2,128)(2,1)S(1)}, bf16[4,12,2,768]{3,2,1,0:T(2,128)(2,1)S(1)}, u32[]{:S(2)}, u32[]{:S(2)}) collective-permute-start(bf16[4,12,2,768]{3,2,1,0:T(2,128)(2,1)S(1)} %get-tuple-element.63), channel_id=1, source_target_pairs={{0,5},{1,4},{2,7},{3,6},{4,1},{5,0},{6,3},{7,2},{8,13},{9,12},{10,... | collective-permute-start | bytes 442376 | tf_op jit(solution)/shard_map/ppermute | solution.py:312
  8.5 3.1 %collective-permute-start.4 = (bf16[4,12,2,768]{3,2,1,0:T(2,128)(2,1)S(1)}, bf16[4,12,2,768]{3,2,1,0:T(2,128)(2,1)S(1)}, u32[]{:S(2)}, u32[]{:S(2)}) collective-permute-start(bf16[4,12,2,768]{3,2,1,0:T(2,128)(2,1)S(1)} %get-tuple-element.64), channel_id=1, source_target_pairs={{0,7},{1,6},{2,5},{3,4},{4,3},{5,2},{6,1},{7,0},{8,15},{9,14},{10,... | collective-permute-start | bytes 442376 | tf_op jit(solution)/shard_map/ppermute | solution.py:312
  11.6 0.0 collective-permute-done
  11.6 1.1 %collective-permute-start.6 = (bf16[4,12,2,768]{3,2,1,0:T(2,128)(2,1)S(1)}, bf16[4,12,2,768]{3,2,1,0:T(2,128)(2,1)S(1)}, u32[]{:S(2)}, u32[]{:S(2)}) collective-permute-start(bf16[4,12,2,768]{3,2,1,0:T(2,128)(2,1)S(1)} %get-tuple-element.68), channel_id=1, source_target_pairs={{0,3},{1,2},{2,1},{3,0},{4,7},{5,6},{6,5},{7,4},{8,11},{9,10},{10,... | collective-permute-start | bytes 442376 | tf_op jit(solution)/shard_map/ppermute | solution.py:312
  12.7 0.9 %collective-permute-done.1 = bf16[4,12,2,768]{3,2,1,0:T(2,128)(2,1)S(1)} collective-permute-done((bf16[4,12,2,768]{3,2,1,0:T(2,128)(2,1)S(1)}, bf16[4,12,2,768]{3,2,1,0:T(2,128)(2,1)S(1)}, u32[]{:S(2)}, u32[]{:S(2)}) %collective-permute-start.1) | collective-permute-done | bytes 147488 | tf_op jit(solution)/shard_map/ppermute | solution.py:312
  13.7 0.0 collective-permute-start.5
  13.7 0.8 %distances.4 = (f32[1,128]{1,0:T(1,128)S(1)}, f32[4,144,128]{2,1,0:T(8,128)S(1)}, f32[4,144,128]{2,1,0:T(8,128)S(1)}, f32[4,144,128]{2,1,0:T(8,128)S(1)}, f32[144,128]{1,0:T(8,128)S(1)}) custom-call(bf16[4,144,128]{2,1,0:T(8,128)(2,1)S(1)} %bitcast.55, bf16[4,144,128]{2,1,0:T(8,128)(2,1)S(1)} %bitcast.56, bf16[4,144,128]{2,1,0:T(8,128)(2,1)S(1)} %bitcast.57, ...), custom_call_target="tpu_custom_call" | custom-call | tf_op jit(solution)/shard_map/distances/pallas_call | solution.py:322
  14.5 0.4 collective-permute-done.2
  14.9 0.6 distances.5
  15.5 3.3 %collective-permute-done.3 = bf16[4,12,2,768]{3,2,1,0:T(2,128)(2,1)S(1)} collective-permute-done((bf16[4,12,2,768]{3,2,1,0:T(2,128)(2,1)S(1)}, bf16[4,12,2,768]{3,2,1,0:T(2,128)(2,1)S(1)}, u32[]{:S(2)}, u32[]{:S(2)}) %collective-permute-start.3) | collective-permute-done | bytes 147488 | tf_op jit(solution)/shard_map/ppermute | solution.py:312
  18.8 0.2 collective-permute-done.4
  19.0 1.5 %distances.6 = (f32[2,128]{1,0:T(2,128)S(1)}, f32[4,144,128]{2,1,0:T(8,128)S(1)}, f32[4,144,128]{2,1,0:T(8,128)S(1)}) custom-call(f32[4,144,128]{2,1,0:T(8,128)S(1)} %get-tuple-element.57.refs_0_.refs_1_.refs_2_, f32[4,144,128]{2,1,0:T(8,128)S(1)} %get-tuple-element.58.refs_1_.refs_2_.refs_3_, f32[4,144,128]{2,1,0:T(8,128)S(1)} %get-tuple-element.59.refs_2_.refs_3_.refs_4_, ...), custom_call_target="tpu_custom_call" | custom-call | tf_op jit(solution)/shard_map/distances/pallas_call | solution.py:322
  20.5 0.0 collective-permute-done.6
  20.5 0.0 collective-permute-done.5
  20.5 2.0 %distances.7 = (f32[8,128]{1,0:T(8,128)S(1)}, f32[4,144,128]{2,1,0:T(8,128)S(1)}, f32[4,144,128]{2,1,0:T(8,128)S(1)}) custom-call(f32[4,144,128]{2,1,0:T(8,128)S(1)} %get-tuple-element.57.refs_0_.refs_1_.refs_2_, f32[4,144,128]{2,1,0:T(8,128)S(1)} %get-tuple-element.58.refs_1_.refs_2_.refs_3_, f32[4,144,128]{2,1,0:T(8,128)S(1)} %get-tuple-element.59.refs_2_.refs_3_.refs_4_, ...), custom_call_target="tpu_custom_call" | custom-call | tf_op jit(solution)/shard_map/distances/pallas_call | solution.py:322
  22.5 0.1 collective-permute-start.7
  22.6 1.2 %collective-permute-done.7 = f32[8,128]{1,0:T(8,128)S(1)} collective-permute-done((f32[8,128]{1,0:T(8,128)S(1)}, f32[8,128]{1,0:T(8,128)S(1)}, u32[]{:S(2)}, u32[]{:S(2)}) %collective-permute-start.7) | collective-permute-done | bytes 4128 | tf_op jit(solution)/shard_map/ppermute | solution.py:333
  23.7 19.8 %all_to_all.5.refs_0_ = f32[16,8,128]{2,1,0:T(8,128)S(1)} all-to-all(f32[16,8,128]{2,1,0:T(8,128)S(1)} %broadcast_in_dim.2), channel_id=1, replica_groups={{0,16,32,48,64,80,96,112,128,144,160,176,192,208,224,240},{8,24,40,56,7..., dimensions={0} | all-to-all | bytes 131072 | tf_op jit(solution)/shard_map/all_to_all | solution.py:336
  43.6 3.4 %gradients.2 = (f32[592,128]{1,0:T(8,128)S(1)}, f32[592,128]{1,0:T(8,128)S(1)}, f32[592,128]{1,0:T(8,128)S(1)}, f32[4,144,128]{2,1,0:T(8,128)S(1)}, f32[4,144,12...) custom-call(f32[16,8,128]{2,1,0:T(8,128)S(1)} %all_to_all.5.refs_0_,, ...), custom_call_target="tpu_custom_call" | custom-call | tf_op jit(solution)/shard_map/gradients/pallas_call | solution.py:342
  47.0 2.8 %collective-permute-start.11 = (f16[592,128]{1,0:T(8,128)(2,1)S(1)}, f16[592,128]{1,0:T(8,128)(2,1)S(1)}, u32[]{:S(2)}, u32[]{:S(2)}) collective-permute-start(f16[592,128]{1,0:T(8,128)(2,1)S(1)} %convert_element_type.48), channel_id=1, source_target_pairs={{0,5},{1,4},{2,7},{3,6},{4,1},{5,0},{6,3},{7,2},{8,13},{9,12},{10,... | collective-permute-start | bytes 454664 | tf_op jit(solution)/shard_map/ppermute | solution.py:356
  49.9 2.1 %collective-permute-start.9 = (f16[592,128]{1,0:T(8,128)(2,1)S(1)}, f16[592,128]{1,0:T(8,128)(2,1)S(1)}, u32[]{:S(2)}, u32[]{:S(2)}) collective-permute-start(f16[592,128]{1,0:T(8,128)(2,1)S(1)} %convert_element_type.44), channel_id=1, source_target_pairs={{0,6},{1,7},{2,4},{3,5},{4,2},{5,3},{6,0},{7,1},{8,14},{9,15},{10,... | collective-permute-start | bytes 454664 | tf_op jit(solution)/shard_map/ppermute | solution.py:356
  52.0 2.6 %gradients.3 = (f32[592,128]{1,0:T(8,128)S(1)}, f32[592,128]{1,0:T(8,128)S(1)}, f32[592,128]{1,0:T(8,128)S(1)}, f32[592,128]{1,0:T(8,128)S(1)}, f32[592,128]{1,0:T(8,128)S(1)}) custom-call(f32[768,128]{1,0:T(8,128)S(1)} %get-tuple-element.76.refs_0_, f32[16,128]{1,0:T(8,128)S(1)} %get-tuple-element.77.refs_1_, ...), custom_call_target="tpu_custom_call" | custom-call | tf_op jit(solution)/shard_map/gradients/pallas_call | solution.py:342
  54.7 1.4 %collective-permute-start.8 = (f16[592,128]{1,0:T(8,128)(2,1)S(1)}, f16[592,128]{1,0:T(8,128)(2,1)S(1)}, u32[]{:S(2)}, u32[]{:S(2)}) collective-permute-start(f16[592,128]{1,0:T(8,128)(2,1)S(1)} %convert_element_type.42), channel_id=1, source_target_pairs={{0,4},{1,5},{2,6},{3,7},{4,0},{5,1},{6,2},{7,3},{8,12},{9,13},{10,... | collective-permute-start | bytes 454664 | tf_op jit(solution)/shard_map/ppermute | solution.py:356
  56.1 1.3 %collective-permute-start.14 = (f16[592,128]{1,0:T(8,128)(2,1)S(1)}, f16[592,128]{1,0:T(8,128)(2,1)S(1)}, u32[]{:S(2)}, u32[]{:S(2)}) collective-permute-start(f16[592,128]{1,0:T(8,128)(2,1)S(1)} %convert_element_type.54), channel_id=1, source_target_pairs={{0,3},{1,2},{2,1},{3,0},{4,7},{5,6},{6,5},{7,4},{8,11},{9,10},{10,... | collective-permute-start | bytes 454664 | tf_op jit(solution)/shard_map/ppermute | solution.py:356
  57.5 0.3 collective-permute-start.13
  57.8 0.0 collective-permute-done.11
  57.8 1.9 %collective-permute-start.12 = (f16[592,128]{1,0:T(8,128)(2,1)S(1)}, f16[592,128]{1,0:T(8,128)(2,1)S(1)}, u32[]{:S(2)}, u32[]{:S(2)}) collective-permute-start(f16[592,128]{1,0:T(8,128)(2,1)S(1)} %convert_element_type.50), channel_id=1, source_target_pairs={{0,7},{1,6},{2,5},{3,4},{4,3},{5,2},{6,1},{7,0},{8,15},{9,14},{10,... | collective-permute-start | bytes 454664 | tf_op jit(solution)/shard_map/ppermute | solution.py:356
  59.7 0.0 collective-permute-done.9
  59.7 1.6 %collective-permute-start.10 = (f16[592,128]{1,0:T(8,128)(2,1)S(1)}, f16[592,128]{1,0:T(8,128)(2,1)S(1)}, u32[]{:S(2)}, u32[]{:S(2)}) collective-permute-start(f16[592,128]{1,0:T(8,128)(2,1)S(1)} %convert_element_type.46), channel_id=1, source_target_pairs={{0,2},{1,3},{2,0},{3,1},{4,6},{5,7},{6,4},{7,5},{8,10},{9,11},{10,... | collective-permute-start | bytes 454664 | tf_op jit(solution)/shard_map/ppermute | solution.py:356
  61.3 1.2 %collective-permute-done.8 = f16[592,128]{1,0:T(8,128)(2,1)S(1)} collective-permute-done((f16[592,128]{1,0:T(8,128)(2,1)S(1)}, f16[592,128]{1,0:T(8,128)(2,1)S(1)}, u32[]{:S(2)}, u32[]{:S(2)}) %collective-permute-start.8) | collective-permute-done | bytes 151584 | tf_op jit(solution)/shard_map/ppermute | solution.py:356
  62.5 1.8 %collective-permute-done.14 = f16[592,128]{1,0:T(8,128)(2,1)S(1)} collective-permute-done((f16[592,128]{1,0:T(8,128)(2,1)S(1)}, f16[592,128]{1,0:T(8,128)(2,1)S(1)}, u32[]{:S(2)}, u32[]{:S(2)}) %collective-permute-start.14) | collective-permute-done | bytes 151584 | tf_op jit(solution)/shard_map/ppermute | solution.py:356
  64.3 0.0 collective-permute-done.13
  64.4 3.7 %collective-permute-done.12 = f16[592,128]{1,0:T(8,128)(2,1)S(1)} collective-permute-done((f16[592,128]{1,0:T(8,128)(2,1)S(1)}, f16[592,128]{1,0:T(8,128)(2,1)S(1)}, u32[]{:S(2)}, u32[]{:S(2)}) %collective-permute-start.12) | collective-permute-done | bytes 151584 | tf_op jit(solution)/shard_map/ppermute | solution.py:356
  68.1 0.0 collective-permute-done.10
  68.2 1.5 %restore.1 = f32[4608,128]{1,0:T(8,128)} custom-call(f32[592,128]{1,0:T(8,128)S(1)} %get-tuple-element.83.refs_0_, f32[592,128]{1,0:T(8,128)S(1)} %convert_element_type.43.refs_1_, f32[592,128]{1,0:T(8,128)S(1)} %convert_element_type.45.refs_2_, f32[592,128]{1,0:T(8,128)S(1)} %convert_element_type.47.refs_3_, f32[592,128]{1,0:T(8,128)S(1)} %convert_element_type.49.refs_4_, ...), custom_call_target="tpu_custom_call" | custom-call | tf_op jit(solution)/shard_map/restore/pallas_call | solution.py:358
  (16 shorter events, 0.3 us)
Async XLA Ops:
  2.0 9.6 %collective-permute-start = (bf16[4,12,2,768]{3,2,1,0:T(2,128)(2,1)S(1)}, bf16[4,12,2,768]{3,2,1,0:T(2,128)(2,1)S(1)}, u32[]{:S(2)}, u32[]{:S(2)}) collective-permute-start(bf16[4,12,2,768]{3,2,1,0:T(2,128)(2,1)S(1)} %get-tuple-element.51), channel_id=1, source_target_pairs={{0,4},{1,5},{2,6},{3,7},{4,0},{5,1},{6,2},{7,3},{8,12},{9,13},{10,... | collective-permute-start | bytes 442376 | tf_op jit(solution)/shard_map/ppermute | solution.py:312
  4.3 9.4 %collective-permute-start.1 = (bf16[4,12,2,768]{3,2,1,0:T(2,128)(2,1)S(1)}, bf16[4,12,2,768]{3,2,1,0:T(2,128)(2,1)S(1)}, u32[]{:S(2)}, u32[]{:S(2)}) collective-permute-start(bf16[4,12,2,768]{3,2,1,0:T(2,128)(2,1)S(1)} %get-tuple-element.54), channel_id=1, source_target_pairs={{0,6},{1,7},{2,4},{3,5},{4,2},{5,3},{6,0},{7,1},{8,14},{9,15},{10,... | collective-permute-start | bytes 442376 | tf_op jit(solution)/shard_map/ppermute | solution.py:312
  6.6 8.3 %collective-permute-start.2 = (bf16[4,12,2,768]{3,2,1,0:T(2,128)(2,1)S(1)}, bf16[4,12,2,768]{3,2,1,0:T(2,128)(2,1)S(1)}, u32[]{:S(2)}, u32[]{:S(2)}) collective-permute-start(bf16[4,12,2,768]{3,2,1,0:T(2,128)(2,1)S(1)} %get-tuple-element.60), channel_id=1, source_target_pairs={{0,2},{1,3},{2,0},{3,1},{4,6},{5,7},{6,4},{7,5},{8,10},{9,11},{10,... | collective-permute-start | bytes 442376 | tf_op jit(solution)/shard_map/ppermute | solution.py:312
  7.4 11.4 %collective-permute-start.3 = (bf16[4,12,2,768]{3,2,1,0:T(2,128)(2,1)S(1)}, bf16[4,12,2,768]{3,2,1,0:T(2,128)(2,1)S(1)}, u32[]{:S(2)}, u32[]{:S(2)}) collective-permute-start(bf16[4,12,2,768]{3,2,1,0:T(2,128)(2,1)S(1)} %get-tuple-element.63), channel_id=1, source_target_pairs={{0,5},{1,4},{2,7},{3,6},{4,1},{5,0},{6,3},{7,2},{8,13},{9,12},{10,... | collective-permute-start | bytes 442376 | tf_op jit(solution)/shard_map/ppermute | solution.py:312
  8.5 10.5 %collective-permute-start.4 = (bf16[4,12,2,768]{3,2,1,0:T(2,128)(2,1)S(1)}, bf16[4,12,2,768]{3,2,1,0:T(2,128)(2,1)S(1)}, u32[]{:S(2)}, u32[]{:S(2)}) collective-permute-start(bf16[4,12,2,768]{3,2,1,0:T(2,128)(2,1)S(1)} %get-tuple-element.64), channel_id=1, source_target_pairs={{0,7},{1,6},{2,5},{3,4},{4,3},{5,2},{6,1},{7,0},{8,15},{9,14},{10,... | collective-permute-start | bytes 442376 | tf_op jit(solution)/shard_map/ppermute | solution.py:312
  11.6 8.9 %collective-permute-start.6 = (bf16[4,12,2,768]{3,2,1,0:T(2,128)(2,1)S(1)}, bf16[4,12,2,768]{3,2,1,0:T(2,128)(2,1)S(1)}, u32[]{:S(2)}, u32[]{:S(2)}) collective-permute-start(bf16[4,12,2,768]{3,2,1,0:T(2,128)(2,1)S(1)} %get-tuple-element.68), channel_id=1, source_target_pairs={{0,3},{1,2},{2,1},{3,0},{4,7},{5,6},{6,5},{7,4},{8,11},{9,10},{10,... | collective-permute-start | bytes 442376 | tf_op jit(solution)/shard_map/ppermute | solution.py:312
  13.7 6.8 %collective-permute-start.5 = (bf16[4,12,2,768]{3,2,1,0:T(2,128)(2,1)S(1)}, bf16[4,12,2,768]{3,2,1,0:T(2,128)(2,1)S(1)}, u32[]{:S(2)}, u32[]{:S(2)}) collective-permute-start(bf16[4,12,2,768]{3,2,1,0:T(2,128)(2,1)S(1)} %get-tuple-element.67), channel_id=1, source_target_pairs={{0,1},{1,0},{2,3},{3,2},{4,5},{5,4},{6,7},{7,6},{8,9},{9,8},{10,11... | collective-permute-start | bytes 442376 | tf_op jit(solution)/shard_map/ppermute | solution.py:312
  22.5 1.2 %collective-permute-start.7 = (f32[8,128]{1,0:T(8,128)S(1)}, f32[8,128]{1,0:T(8,128)S(1)}, u32[]{:S(2)}, u32[]{:S(2)}) collective-permute-start(f32[8,128]{1,0:T(8,128)S(1)} %get-tuple-element.72), channel_id=1, source_target_pairs={{0,8},{8,0},{16,24},{24,16},{32,40},{40,32},{48,56},{56,48},{64,72... | collective-permute-start | bytes 12296 | tf_op jit(solution)/shard_map/ppermute | solution.py:333
  47.0 10.8 %collective-permute-start.11 = (f16[592,128]{1,0:T(8,128)(2,1)S(1)}, f16[592,128]{1,0:T(8,128)(2,1)S(1)}, u32[]{:S(2)}, u32[]{:S(2)}) collective-permute-start(f16[592,128]{1,0:T(8,128)(2,1)S(1)} %convert_element_type.48), channel_id=1, source_target_pairs={{0,5},{1,4},{2,7},{3,6},{4,1},{5,0},{6,3},{7,2},{8,13},{9,12},{10,... | collective-permute-start | bytes 454664 | tf_op jit(solution)/shard_map/ppermute | solution.py:356
  49.9 9.8 %collective-permute-start.9 = (f16[592,128]{1,0:T(8,128)(2,1)S(1)}, f16[592,128]{1,0:T(8,128)(2,1)S(1)}, u32[]{:S(2)}, u32[]{:S(2)}) collective-permute-start(f16[592,128]{1,0:T(8,128)(2,1)S(1)} %convert_element_type.44), channel_id=1, source_target_pairs={{0,6},{1,7},{2,4},{3,5},{4,2},{5,3},{6,0},{7,1},{8,14},{9,15},{10,... | collective-permute-start | bytes 454664 | tf_op jit(solution)/shard_map/ppermute | solution.py:356
  54.7 7.8 %collective-permute-start.8 = (f16[592,128]{1,0:T(8,128)(2,1)S(1)}, f16[592,128]{1,0:T(8,128)(2,1)S(1)}, u32[]{:S(2)}, u32[]{:S(2)}) collective-permute-start(f16[592,128]{1,0:T(8,128)(2,1)S(1)} %convert_element_type.42), channel_id=1, source_target_pairs={{0,4},{1,5},{2,6},{3,7},{4,0},{5,1},{6,2},{7,3},{8,12},{9,13},{10,... | collective-permute-start | bytes 454664 | tf_op jit(solution)/shard_map/ppermute | solution.py:356
  56.1 8.2 %collective-permute-start.14 = (f16[592,128]{1,0:T(8,128)(2,1)S(1)}, f16[592,128]{1,0:T(8,128)(2,1)S(1)}, u32[]{:S(2)}, u32[]{:S(2)}) collective-permute-start(f16[592,128]{1,0:T(8,128)(2,1)S(1)} %convert_element_type.54), channel_id=1, source_target_pairs={{0,3},{1,2},{2,1},{3,0},{4,7},{5,6},{6,5},{7,4},{8,11},{9,10},{10,... | collective-permute-start | bytes 454664 | tf_op jit(solution)/shard_map/ppermute | solution.py:356
  57.5 6.9 %collective-permute-start.13 = (f16[592,128]{1,0:T(8,128)(2,1)S(1)}, f16[592,128]{1,0:T(8,128)(2,1)S(1)}, u32[]{:S(2)}, u32[]{:S(2)}) collective-permute-start(f16[592,128]{1,0:T(8,128)(2,1)S(1)} %convert_element_type.52), channel_id=1, source_target_pairs={{0,1},{1,0},{2,3},{3,2},{4,5},{5,4},{6,7},{7,6},{8,9},{9,8},{10,11... | collective-permute-start | bytes 454664 | tf_op jit(solution)/shard_map/ppermute | solution.py:356
  57.8 10.3 %collective-permute-start.12 = (f16[592,128]{1,0:T(8,128)(2,1)S(1)}, f16[592,128]{1,0:T(8,128)(2,1)S(1)}, u32[]{:S(2)}, u32[]{:S(2)}) collective-permute-start(f16[592,128]{1,0:T(8,128)(2,1)S(1)} %convert_element_type.50), channel_id=1, source_target_pairs={{0,7},{1,6},{2,5},{3,4},{4,3},{5,2},{6,1},{7,0},{8,15},{9,14},{10,... | collective-permute-start | bytes 454664 | tf_op jit(solution)/shard_map/ppermute | solution.py:356
  59.7 8.4 %collective-permute-start.10 = (f16[592,128]{1,0:T(8,128)(2,1)S(1)}, f16[592,128]{1,0:T(8,128)(2,1)S(1)}, u32[]{:S(2)}, u32[]{:S(2)}) collective-permute-start(f16[592,128]{1,0:T(8,128)(2,1)S(1)} %convert_element_type.46), channel_id=1, source_target_pairs={{0,2},{1,3},{2,0},{3,1},{4,6},{5,7},{6,4},{7,5},{8,10},{9,11},{10,... | collective-permute-start | bytes 454664 | tf_op jit(solution)/shard_map/ppermute | solution.py:356
